TPU v7x, 128 devices: a whole 4x4x4 slice. The times are simulated.
128 devices in a mesh: dp: 16 (over x, z_lo, core), tensor: 8 (over z_hi, y).
Axes of the slice: x: 4, y: 4, z: 4 (z_hi: 2, z_lo: 2; z = z_hi * 2 + z_lo), core: 2. Of those that a mesh axis runs over, the one named last changes fastest.
Arguments:
- act_mant: int32 [16384, 6144], P(('dp', 'tensor')), may hold values from -127 to 127
- act_exp: int32 [16384, 48], P(('dp', 'tensor')), may hold values from -9 to -6
- grad_mant: int32 [16384, 8192], P('dp', 'tensor'), may hold values from -127 to 127
- grad_exp: int32 [128, 8192], P('dp', 'tensor'), may hold values from -14 to -11
Outputs:
- weight_grad: float32 [6144, 8192], P('dp', 'tensor')
All inputs are finite; a program needn't handle non-finite values.
Results may differ from a plain program's by a relative error of at most 0.0003.
Values may be sent and summed in bfloat16 or wider, within the bound.
No kernel may reach another device: no remote copies, remote signals or barrier semaphores. Data moves between devices by JAX's collectives and lax.ppermute only.
A program may use at most 128 MiB of HBM per device.

v0:
```python
import jax
import jax.numpy as jnp
from jax import lax
from jax.sharding import PartitionSpec as P


def widen_rows(mantissa, exponent):
    scale = jnp.exp2(exponent.astype(jnp.float32))
    count = mantissa.shape[0]
    blocks = exponent.shape[1]
    values = mantissa.astype(jnp.float32).reshape(count, blocks, 128) * scale[:, :, None]
    return values.reshape(count, blocks * 128).astype(jnp.bfloat16)


def widen_columns(mantissa, exponent):
    scale = jnp.exp2(exponent.astype(jnp.float32))
    blocks = exponent.shape[0]
    width = exponent.shape[1]
    values = mantissa.astype(jnp.float32).reshape(blocks, 128, width) * scale[:, None, :]
    return values.reshape(blocks * 128, width).astype(jnp.bfloat16)


def contract_tokens(left, right):
    return lax.dot_general(
        left, right, (((0,), (0,)), ((), ())), preferred_element_type=jnp.float32
    )


def body(act_mant, act_exp, grad_mant, grad_exp):
    local_rows = widen_rows(act_mant, act_exp)
    grad_vals = widen_columns(grad_mant, grad_exp)
    gathered = lax.all_gather(local_rows, "tensor", axis=0, tiled=True)
    return lax.psum_scatter(
        contract_tokens(gathered, grad_vals), "dp", scatter_dimension=0, tiled=True
    )


def solution(mesh):
    return jax.shard_map(
        body,
        mesh=mesh,
        in_specs=(
            P(("dp", "tensor"), None),
            P(("dp", "tensor"), None),
            P("dp", "tensor"),
            P("dp", "tensor"),
        ),
        out_specs=P("dp", "tensor"),
        check_vma=False,
    )
```

profile of v0, /device:TPU:6, one launch (start us, length us, event | category | flops | bytes accessed | tf_op | source)
XLA Modules:
  0.0 444.3 jit_solution(4617438749836673684)
XLA Ops:
  6.5 0.0 copy-start
  6.5 0.0 all-gather.2.cloned.1.call-start
  6.5 0.9 multiply_exponential_fusion.1
  7.4 0.1 copy.5
  7.5 0.9 mul.22
  8.4 0.0 copy-done
  8.4 0.0 copy-start.1
  8.4 2.2 fusion.1
  10.7 0.0 all-gather.2.cloned.1.call-update
  10.7 0.0 reduce-scatter.2.cloned.1.call-start
  10.8 0.0 copy-done.1
  10.8 2.8 fusion
  13.6 147.1 %all-gather.2.cloned.1.call-done = bf16[1024,6144]{1,0:T(8,128)(2,1)} async-done(((bf16[128,6144]{1,0:T(8,128)(2,1)}), bf16[1024,6144]{1,0:T(8,128)(2,1)}) %all-gather.2.cloned.1.call-update) | async-done | bytes 12582928 | tf_op jit(solution)/shard_map/all_gather | solution.py:32
  160.7 20.8 %fusion.2 = f32[6144,1024]{1,0:T(8,128)} fusion(bf16[1024,6144]{1,0:T(8,128)(2,1)} %all-gather.2.cloned.1.call-done, bf16[1024,1024]{1,0:T(8,128)(2,1)S(1)} %fusion), kind=kOutput, calls=%fused_computation.6 | convolution fusion | flops 12884901888 | bytes 39845888 | tf_op jit(solution)/shard_map/dot_general | solution.py:24
  181.5 0.0 reduce-scatter.2.cloned.1.call-update
  181.5 255.9 %reduce-scatter.2.cloned.1.call-done = f32[384,1024]{1,0:T(8,128)} async-done(((f32[6144,1024]{1,0:T(8,128)}), f32[384,1024]{1,0:T(8,128)}) %reduce-scatter.2.cloned.1.call-update) | async-done | bytes 1572880 | tf_op jit(solution)/shard_map/reduce_scatter | solution.py:33
  (1 shorter events, 0.0 us)
Async XLA Ops:
  6.5 1.9 copy-start
  6.5 154.1 %all-gather.2.cloned.1.call-start = ((), (), s32[]{:S(2)}) async-start(), calls=%async_computation.1 | async-start | bytes 14155776 | tf_op jit(solution)/shard_map/all_gather | solution.py:32
  8.4 2.3 copy-start.1
  10.7 426.8 %reduce-scatter.2.cloned.1.call-start = ((), (), s32[]{:S(2)}) async-start(), calls=%async_computation.2 | async-start | bytes 26738688 | tf_op jit(solution)/shard_map/reduce_scatter | solution.py:33
Sparse Core Ops, SparseCore 0:
  10.8 149.8 all-gather.1
  181.6 255.7 reduce-scatter.1
where the time goes:
time: 453 us; the launch traced here: 444 us
  waiting for transfers between devices  403 us (89%)
  matrix products  20.8 us (5%)
  between operations  13.4 us (3%)
  other arithmetic  5.96 us (1%)
    reduce_scatter x1, waiting for transfers between devices, body(): lax.psum_scatter(contract_tokens(gathered, grad_vals), 'dp', scatter_dime...  256 us
    all_gather x1, waiting for transfers between devices, body(): gathered = lax.all_gather(local_rows, 'tensor', axis=0, tiled=True)  147 us
    dot_general x1, matrix products, contract_tokens(): lax.dot_general(left, right, (((0,), (0,)), ((), ())), preferred_element_...  20.8 us
  transfers between devices with their start and end apart: 2, of which 2 were waited for; matrix products, arithmetic and copies ran while one was open for 1% of the time, Pallas kernels for 0%

commit v1 on v0

v1 whole, which is shorter than its diff:
```python
import jax
import jax.numpy as jnp
from jax import lax
from jax.experimental import pallas as pl
from jax.experimental.pallas import tpu as pltpu
from jax.sharding import PartitionSpec as P

AXES = ("dp", "tensor")
BLOCK = 128
PARTS = 3


def place(index):
    dp, tensor = index // 8, index % 8
    return dp // 4, tensor % 4, (tensor // 4) * 2 + (dp // 2) % 2, dp % 2


def index_of(x, y, z, core):
    return ((x * 2 + z % 2) * 2 + core) * 8 + (z // 2) * 4 + y


def send(value, x=0, y=0, z=0, core=0):
    pairs = []
    for source in range(128):
        sx, sy, sz, sc = place(source)
        pairs.append((source, index_of((sx + x) % 4, (sy + y) % 4, sz ^ z, sc ^ core)))
    return lax.ppermute(value, AXES, pairs)


def act_kernel(where, mant, scale, out):
    x, z_lo, core = where[0], where[1], where[2]
    for owner in range(16):
        ox, oz, oc = owner // 4, (owner // 2) % 2, owner % 2
        slot = lax.rem(ox - x + 4, 4)
        for k in range(PARTS):
            b = owner * PARTS + k
            values = mant[:, b * BLOCK : (b + 1) * BLOCK].astype(jnp.float32) * scale[:, b : b + 1]
            lanes = pl.ds(pl.multiple_of(slot * BLOCK, BLOCK), BLOCK)
            out[oc ^ core, oz ^ z_lo, k, :, lanes] = values.astype(jnp.bfloat16)


def widen_act(mant, exponent, where):
    tokens = mant.shape[0]
    return pl.pallas_call(
        act_kernel,
        out_shape=jax.ShapeDtypeStruct((2, 2, PARTS, tokens, 4 * BLOCK), jnp.bfloat16),
        in_specs=[
            pl.BlockSpec(memory_space=pltpu.SMEM),
            pl.BlockSpec(memory_space=pltpu.VMEM),
            pl.BlockSpec(memory_space=pltpu.VMEM),
        ],
        out_specs=pl.BlockSpec(memory_space=pltpu.VMEM),
        compiler_params=pltpu.CompilerParams(vmem_limit_bytes=32 * 1024 * 1024),
    )(where, mant, jnp.exp2(exponent.astype(jnp.float32)))


def grad_kernel(order, mant, scale, out):
    out[0] = (mant[...].astype(jnp.float32) * scale[0]).astype(jnp.bfloat16)


def widen_grad(mant, exponent, order):
    blocks, width = exponent.shape
    scale = jnp.exp2(exponent.astype(jnp.float32)).reshape(blocks, 1, width)
    return pl.pallas_call(
        grad_kernel,
        out_shape=jax.ShapeDtypeStruct((blocks, BLOCK, width), jnp.bfloat16),
        grid_spec=pltpu.PrefetchScalarGridSpec(
            num_scalar_prefetch=1,
            grid=(blocks,),
            in_specs=[
                pl.BlockSpec((BLOCK, width), lambda i, order: (order[i], 0)),
                pl.BlockSpec((1, 1, width), lambda i, order: (order[i], 0, 0)),
            ],
            out_specs=pl.BlockSpec((1, BLOCK, width), lambda i, order: (i, 0, 0)),
        ),
        compiler_params=pltpu.CompilerParams(vmem_limit_bytes=32 * 1024 * 1024),
    )(order, mant, scale)


def contract(left, right):
    return lax.dot_general(
        left, right, (((0,), (0,)), ((), ())), preferred_element_type=jnp.float32
    )


def body(act_mant, act_exp, grad_mant, grad_exp):
    dp, tensor = lax.axis_index("dp"), lax.axis_index("tensor")
    x, z_lo, core = dp // 4, (dp // 2) % 2, dp % 2
    z_hi, y = tensor // 4, tensor % 4

    act = widen_act(act_mant, act_exp, jnp.stack([x, z_lo, core]).astype(jnp.int32))
    order = jnp.stack(
        [(z_hi ^ flip) * 4 + (y + step) % 4 for step in range(4) for flip in range(2)]
    ).astype(jnp.int32)
    own_grad = widen_grad(grad_mant, grad_exp, order).reshape(4, 2, BLOCK, -1)

    other = send(act[1], core=1)
    grad_c = send(own_grad, core=1)
    grad_z = send(own_grad, z=1)
    grad_zc = send(grad_z, core=1)
    grads = jnp.stack(
        [
            jnp.stack([own_grad, grad_c], axis=2),
            jnp.stack([grad_z, grad_zc], axis=2),
        ],
        axis=1,
    ).reshape(4, 8 * BLOCK, -1)

    width = grads.shape[-1]
    half = width // 2
    rows = []
    for k in range(PARTS):
        here, there = (
            jnp.concatenate([act[0, flip, k], other[flip, k]], axis=0) for flip in range(2)
        )
        piece = jnp.concatenate(
            [here, send(here, z=2), send(there, z=1), send(there, z=3)], axis=0
        )
        mid = piece.shape[0] // 2
        behind = send(piece, y=1)
        ahead = send(piece, y=3)
        far = jnp.concatenate([send(behind[:mid], y=1), send(ahead[mid:], y=3)], axis=0)
        total = contract(piece, grads[0]) + contract(ahead, grads[1])
        total = total + contract(behind, grads[3]) + contract(far, grads[2])
        total = total.reshape(4, BLOCK, width)
        first = send(total[2, :, :half], x=1)
        second = send(total[2, :, half:], x=3)
        to_next = jnp.concatenate([total[1, :, :half] + first, total[1, :, half:]], axis=1)
        to_last = jnp.concatenate([total[3, :, :half], total[3, :, half:] + second], axis=1)
        rows.append(total[0] + send(to_next, x=1) + send(to_last, x=3))
    return jnp.concatenate(rows, axis=0)


def solution(mesh):
    return jax.shard_map(
        body,
        mesh=mesh,
        in_specs=(
            P(("dp", "tensor"), None),
            P(("dp", "tensor"), None),
            P("dp", "tensor"),
            P("dp", "tensor"),
        ),
        out_specs=P("dp", "tensor"),
        check_vma=False,
    )
```

time: 453 us -> 243 us (0.54); the launches traced: 444 us -> 243 us
  waiting for transfers between devices: 403 us -> 164 us
  starting transfers between devices: 0.04 us -> 50.1 us
  between operations: 13.4 us -> 0.59 us
  matrix products: 20.8 us -> 15.7 us
    reduce_scatter x1 -> x0, waiting for transfers between devices: 256 us -> none  [body(): lax.psum_scatter(contract_tokens(gathered, grad_vals), 'dp', scatter_dime...]
    ppermute x0 -> x37, waiting for transfers between devices: none -> 164 us  [send(): return lax.ppermute(value, AXES, pairs)]
    all_gather x1 -> x0, waiting for transfers between devices: 147 us -> none  [body(): gathered = lax.all_gather(local_rows, 'tensor', axis=0, tiled=True)]
    ppermute x0 -> x37, starting transfers between devices: none -> 50.1 us  [send(): return lax.ppermute(value, AXES, pairs)]
    dot_general x1 -> x12, matrix products: 20.8 us -> 15.7 us  [contract(): lax.dot_general(left, right, (((0,), (0,)), ((), ())), preferred_element_...]
  transfers between devices with their start and end apart: 2 -> 37, of which waited for: 2 -> 21; matrix products, arithmetic and copies ran while one was open for 1% -> 8% of each run, Pallas kernels for 0% -> 0%
where the time goes in v1:
time: 243 us
  waiting for transfers between devices  164 us (67%)
  starting transfers between devices  50.1 us (21%)
  matrix products  15.7 us (6%)
  local copies, waits for them, and re-layouts  5.12 us (2%)
  other arithmetic  4.28 us (2%)
  Pallas kernels  2.56 us (1%)
    ppermute x37, waiting for transfers between devices, send(): return lax.ppermute(value, AXES, pairs)  164 us
    ppermute x37, starting transfers between devices, send(): return lax.ppermute(value, AXES, pairs)  50.1 us
    dot_general x12, matrix products, contract(): lax.dot_general(left, right, (((0,), (0,)), ((), ())), preferred_element_...  15.7 us
  transfers between devices with their start and end apart: 37, of which 21 were waited for; matrix products, arithmetic and copies ran while one was open for 8% of the time, Pallas kernels for 0%

profile of v1, /device:TPU:6, one launch (start us, length us, event | category | flops | bytes accessed | tf_op | source)
XLA Modules:
  0.0 242.6 jit_solution(13294101103976412934)
XLA Ops:
  1.0 1.9 copy-done.1
  4.8 2.2 copy-done
  8.0 2.0 collective-permute-start.5
  10.4 4.0 %collective-permute-start.3 = (bf16[256,512]{1,0:T(8,128)(2,1)S(1)}, bf16[256,512]{1,0:T(8,128)(2,1)S(1)}, u32[]{:S(2)}, u32[]{:S(2)}) collective-permute-start(bf16[256,512]{1,0:T(8,128)(2,1)S(1)} %pad_maximum_fusion.9), channel_id=1, source_target_pairs={{0,20},{1,21},{2,22},{3,23},{4,16},{5,17},{6,18},{7,19},{8,28},{9,... | collective-permute-start | bytes 786440 | tf_op jit(solution)/shard_map/ppermute | solution.py:27
  14.6 3.6 %collective-permute-start.15 = (bf16[256,512]{1,0:T(8,128)(2,1)S(1)}, bf16[256,512]{1,0:T(8,128)(2,1)S(1)}, u32[]{:S(2)}, u32[]{:S(2)}) collective-permute-start(bf16[256,512]{1,0:T(8,128)(2,1)S(1)} %pad_maximum_fusion.10), channel_id=1, source_target_pairs={{0,4},{1,5},{2,6},{3,7},{4,0},{5,1},{6,2},{7,3},{8,12},{9,13},{10,... | collective-permute-start | bytes 786440 | tf_op jit(solution)/shard_map/ppermute | solution.py:27
  18.3 53.0 %collective-permute-done.1 = bf16[256,512]{1,0:T(8,128)(2,1)S(1)} collective-permute-done((bf16[256,512]{1,0:T(8,128)(2,1)S(1)}, bf16[256,512]{1,0:T(8,128)(2,1)S(1)}, u32[]{:S(2)}, u32[]{:S(2)}) %collective-permute-start.1) | collective-permute-done | bytes 262176 | tf_op jit(solution)/shard_map/ppermute | solution.py:27
  71.9 3.7 %collective-permute-start.26 = (bf16[256,512]{1,0:T(8,128)(2,1)S(1)}, bf16[256,512]{1,0:T(8,128)(2,1)S(1)}, u32[]{:S(2)}, u32[]{:S(2)}) collective-permute-start(bf16[256,512]{1,0:T(8,128)(2,1)S(1)} %pad_maximum_fusion.12), channel_id=1, source_target_pairs={{0,4},{1,5},{2,6},{3,7},{4,0},{5,1},{6,2},{7,3},{8,12},{9,13},{10,... | collective-permute-start | bytes 786440 | tf_op jit(solution)/shard_map/ppermute | solution.py:27
  76.9 3.6 %collective-permute-done.16 = bf16[256,512]{1,0:T(8,128)(2,1)S(1)} collective-permute-done((bf16[256,512]{1,0:T(8,128)(2,1)S(1)}, bf16[256,512]{1,0:T(8,128)(2,1)S(1)}, u32[]{:S(2)}, u32[]{:S(2)}) %collective-permute-start.16) | collective-permute-done | bytes 262176 | tf_op jit(solution)/shard_map/ppermute | solution.py:27
  80.5 3.0 %collective-permute-start.7 = (bf16[1024,512]{1,0:T(8,128)(2,1)S(1)}, bf16[1024,512]{1,0:T(8,128)(2,1)S(1)}, u32[]{:S(2)}, u32[]{:S(2)}) collective-permute-start(bf16[1024,512]{1,0:T(8,128)(2,1)S(1)} %constant_dynamic-update-slice_fusion), channel_id=1, source_target_pairs={{0,3},{1,0},{2,1},{3,2},{4,7},{5,4},{6,5},{7,6},{8,11},{9,8},{10,9... | collective-permute-start | bytes 3145736 | tf_op jit(solution)/shard_map/ppermute | solution.py:27
  83.5 2.6 %collective-permute-start.28 = (bf16[256,512]{1,0:T(8,128)(2,1)S(1)}, bf16[256,512]{1,0:T(8,128)(2,1)S(1)}, u32[]{:S(2)}, u32[]{:S(2)}) collective-permute-start(bf16[256,512]{1,0:T(8,128)(2,1)S(1)} %pad_maximum_fusion.13), channel_id=1, source_target_pairs={{0,20},{1,21},{2,22},{3,23},{4,16},{5,17},{6,18},{7,19},{8,28},{9,... | collective-permute-start | bytes 786440 | tf_op jit(solution)/shard_map/ppermute | solution.py:27
  86.2 1.9 collective-permute-done.26
  91.5 1.7 collective-permute-done.28
  93.3 10.0 %collective-permute-done.7 = bf16[1024,512]{1,0:T(8,128)(2,1)S(1)} collective-permute-done((bf16[1024,512]{1,0:T(8,128)(2,1)S(1)}, bf16[1024,512]{1,0:T(8,128)(2,1)S(1)}, u32[]{:S(2)}, u32[]{:S(2)}) %collective-permute-start.7) | collective-permute-done | bytes 1048608 | tf_op jit(solution)/shard_map/ppermute | solution.py:27
  103.3 3.6 %collective-permute-start.18 = (bf16[1024,512]{1,0:T(8,128)(2,1)S(1)}, bf16[1024,512]{1,0:T(8,128)(2,1)S(1)}, u32[]{:S(2)}, u32[]{:S(2)}) collective-permute-start(bf16[1024,512]{1,0:T(8,128)(2,1)S(1)} %constant_dynamic-update-slice_fusion.5), channel_id=1, source_target_pairs={{0,3},{1,0},{2,1},{3,2},{4,7},{5,4},{6,5},{7,6},{8,11},{9,8},{10,9... | collective-permute-start | bytes 3145736 | tf_op jit(solution)/shard_map/ppermute | solution.py:27
  106.9 8.5 %collective-permute-done.8 = bf16[1024,512]{1,0:T(8,128)(2,1)S(1)} collective-permute-done((bf16[1024,512]{1,0:T(8,128)(2,1)S(1)}, bf16[1024,512]{1,0:T(8,128)(2,1)S(1)}, u32[]{:S(2)}, u32[]{:S(2)}) %collective-permute-start.8) | collective-permute-done | bytes 1048608 | tf_op jit(solution)/shard_map/ppermute | solution.py:27
  115.8 22.1 %collective-permute-done.19 = bf16[1024,512]{1,0:T(8,128)(2,1)S(1)} collective-permute-done((bf16[1024,512]{1,0:T(8,128)(2,1)S(1)}, bf16[1024,512]{1,0:T(8,128)(2,1)S(1)}, u32[]{:S(2)}, u32[]{:S(2)}) %collective-permute-start.19) | collective-permute-done | bytes 1048608 | tf_op jit(solution)/shard_map/ppermute | solution.py:27
  137.9 1.8 collective-permute-start.29
  140.7 17.9 %collective-permute-done.30 = bf16[1024,512]{1,0:T(8,128)(2,1)S(1)} collective-permute-done((bf16[1024,512]{1,0:T(8,128)(2,1)S(1)}, bf16[1024,512]{1,0:T(8,128)(2,1)S(1)}, u32[]{:S(2)}, u32[]{:S(2)}) %collective-permute-start.30) | collective-permute-done | bytes 1048608 | tf_op jit(solution)/shard_map/ppermute | solution.py:27
  158.9 5.1 %collective-permute-done.29 = bf16[1024,512]{1,0:T(8,128)(2,1)S(1)} collective-permute-done((bf16[1024,512]{1,0:T(8,128)(2,1)S(1)}, bf16[1024,512]{1,0:T(8,128)(2,1)S(1)}, u32[]{:S(2)}, u32[]{:S(2)}) %collective-permute-start.29) | collective-permute-done | bytes 1048608 | tf_op jit(solution)/shard_map/ppermute | solution.py:27
  164.4 2.9 %collective-permute-start.21 = (bf16[512,512]{1,0:T(8,128)(2,1)S(1)}, bf16[512,512]{1,0:T(8,128)(2,1)S(1)}, u32[]{:S(2)}, u32[]{:S(2)}) collective-permute-start(bf16[512,512]{1,0:T(8,128)(2,1)S(1)} %slice.216), channel_id=1, source_target_pairs={{0,3},{1,0},{2,1},{3,2},{4,7},{5,4},{6,5},{7,6},{8,11},{9,8},{10,9... | collective-permute-start | bytes 1572872 | tf_op jit(solution)/shard_map/ppermute | solution.py:27
  175.4 3.3 %collective-permute-start.32 = (bf16[512,512]{1,0:T(8,128)(2,1)S(1)}, bf16[512,512]{1,0:T(8,128)(2,1)S(1)}, u32[]{:S(2)}, u32[]{:S(2)}) collective-permute-start(bf16[512,512]{1,0:T(8,128)(2,1)S(1)} %slice.229), channel_id=1, source_target_pairs={{0,3},{1,0},{2,1},{3,2},{4,7},{5,4},{6,5},{7,6},{8,11},{9,8},{10,9... | collective-permute-start | bytes 1572872 | tf_op jit(solution)/shard_map/ppermute | solution.py:27
  183.3 2.5 %collective-permute-done.20 = bf16[512,512]{1,0:T(8,128)(2,1)S(1)} collective-permute-done((bf16[512,512]{1,0:T(8,128)(2,1)S(1)}, bf16[512,512]{1,0:T(8,128)(2,1)S(1)}, u32[]{:S(2)}, u32[]{:S(2)}) %collective-permute-start.20) | collective-permute-done | bytes 524320 | tf_op jit(solution)/shard_map/ppermute | solution.py:27
  188.1 2.5 %collective-permute-start.22 = (f32[128,512]{1,0:T(8,128)S(1)}, f32[128,512]{1,0:T(8,128)S(1)}, u32[]{:S(2)}, u32[]{:S(2)}) collective-permute-start(f32[128,512]{1,0:T(8,128)S(1)} %get-tuple-element.17), channel_id=1, source_target_pairs={{0,32},{1,33},{2,34},{3,35},{4,36},{5,37},{6,38},{7,39},{8,40},{9,... | collective-permute-start | bytes 786440 | tf_op jit(solution)/shard_map/ppermute | solution.py:27
  196.6 2.5 %collective-permute-start.33 = (f32[128,512]{1,0:T(8,128)S(1)}, f32[128,512]{1,0:T(8,128)S(1)}, u32[]{:S(2)}, u32[]{:S(2)}) collective-permute-start(f32[128,512]{1,0:T(8,128)S(1)} %get-tuple-element.23), channel_id=1, source_target_pairs={{0,32},{1,33},{2,34},{3,35},{4,36},{5,37},{6,38},{7,39},{8,40},{9,... | collective-permute-start | bytes 786440 | tf_op jit(solution)/shard_map/ppermute | solution.py:27
  199.2 3.3 %collective-permute-start.12 = (f32[128,1024]{1,0:T(8,128)S(1)}, f32[128,1024]{1,0:T(8,128)S(1)}, u32[]{:S(2)}, u32[]{:S(2)}) collective-permute-start(f32[128,1024]{1,0:T(8,128)S(1)} %pad_maximum_fusion.2), channel_id=1, source_target_pairs={{0,32},{1,33},{2,34},{3,35},{4,36},{5,37},{6,38},{7,39},{8,40},{9,... | collective-permute-start | bytes 1572872 | tf_op jit(solution)/shard_map/ppermute | solution.py:27
  206.6 3.3 %collective-permute-done.35 = f32[128,512]{1,0:T(8,128)S(1)} collective-permute-done((f32[128,512]{1,0:T(8,128)S(1)}, f32[128,512]{1,0:T(8,128)S(1)}, u32[]{:S(2)}, u32[]{:S(2)}) %collective-permute-start.35) | collective-permute-done | bytes 262176 | tf_op jit(solution)/shard_map/ppermute | solution.py:27
  210.1 7.0 %collective-permute-done.12 = f32[128,1024]{1,0:T(8,128)S(1)} collective-permute-done((f32[128,1024]{1,0:T(8,128)S(1)}, f32[128,1024]{1,0:T(8,128)S(1)}, u32[]{:S(2)}, u32[]{:S(2)}) %collective-permute-start.12) | collective-permute-done | bytes 524320 | tf_op jit(solution)/shard_map/ppermute | solution.py:27
  217.7 3.4 %collective-permute-done.14 = f32[128,1024]{1,0:T(8,128)S(1)} collective-permute-done((f32[128,1024]{1,0:T(8,128)S(1)}, f32[128,1024]{1,0:T(8,128)S(1)}, u32[]{:S(2)}, u32[]{:S(2)}) %collective-permute-start.14) | collective-permute-done | bytes 524320 | tf_op jit(solution)/shard_map/ppermute | solution.py:27
  221.2 7.2 %collective-permute-done.23 = f32[128,1024]{1,0:T(8,128)S(1)} collective-permute-done((f32[128,1024]{1,0:T(8,128)S(1)}, f32[128,1024]{1,0:T(8,128)S(1)}, u32[]{:S(2)}, u32[]{:S(2)}) %collective-permute-start.23) | collective-permute-done | bytes 524320 | tf_op jit(solution)/shard_map/ppermute | solution.py:27
  228.4 4.0 %collective-permute-done.25 = f32[128,1024]{1,0:T(8,128)S(1)} collective-permute-done((f32[128,1024]{1,0:T(8,128)S(1)}, f32[128,1024]{1,0:T(8,128)S(1)}, u32[]{:S(2)}, u32[]{:S(2)}) %collective-permute-start.25) | collective-permute-done | bytes 524320 | tf_op jit(solution)/shard_map/ppermute | solution.py:27
  232.4 3.2 %collective-permute-done.34 = f32[128,1024]{1,0:T(8,128)S(1)} collective-permute-done((f32[128,1024]{1,0:T(8,128)S(1)}, f32[128,1024]{1,0:T(8,128)S(1)}, u32[]{:S(2)}, u32[]{:S(2)}) %collective-permute-start.34) | collective-permute-done | bytes 524320 | tf_op jit(solution)/shard_map/ppermute | solution.py:27
  235.7 5.6 %collective-permute-done.36 = f32[128,1024]{1,0:T(8,128)S(1)} collective-permute-done((f32[128,1024]{1,0:T(8,128)S(1)}, f32[128,1024]{1,0:T(8,128)S(1)}, u32[]{:S(2)}, u32[]{:S(2)}) %collective-permute-start.36) | collective-permute-done | bytes 524320 | tf_op jit(solution)/shard_map/ppermute | solution.py:27
  (113 shorter events, 39.2 us)
Async XLA Ops:
  8.0 83.5 %collective-permute-start.5 = (bf16[4,2,128,1024]{3,2,1,0:T(8,128)(2,1)S(1)}, bf16[4,2,128,1024]{3,2,1,0:T(8,128)(2,1)S(1)}, u32[]{:S(2)}, u32[]{:S(2)}) collective-permute-start(bf16[4,2,128,1024]{3,2,1,0:T(8,128)(2,1)S(1)} %bitcast.138), channel_id=1, source_target_pairs={{0,16},{1,17},{2,18},{3,19},{4,20},{5,21},{6,22},{7,23},{8,24},{9,... | collective-permute-start | bytes 6291464 | tf_op jit(solution)/shard_map/ppermute | solution.py:27
  10.2 61.1 %collective-permute-start.2 = (bf16[256,512]{1,0:T(8,128)(2,1)S(1)}, bf16[256,512]{1,0:T(8,128)(2,1)S(1)}, u32[]{:S(2)}, u32[]{:S(2)}) collective-permute-start(bf16[256,512]{1,0:T(8,128)(2,1)S(1)} %pad_maximum_fusion.9), channel_id=1, source_target_pairs={{0,16},{1,17},{2,18},{3,19},{4,20},{5,21},{6,22},{7,23},{8,24},{9,... | collective-permute-start | bytes 786440 | tf_op jit(solution)/shard_map/ppermute | solution.py:27
  10.4 61.5 %collective-permute-start.3 = (bf16[256,512]{1,0:T(8,128)(2,1)S(1)}, bf16[256,512]{1,0:T(8,128)(2,1)S(1)}, u32[]{:S(2)}, u32[]{:S(2)}) collective-permute-start(bf16[256,512]{1,0:T(8,128)(2,1)S(1)} %pad_maximum_fusion.9), channel_id=1, source_target_pairs={{0,20},{1,21},{2,22},{3,23},{4,16},{5,17},{6,18},{7,19},{8,28},{9,... | collective-permute-start | bytes 786440 | tf_op jit(solution)/shard_map/ppermute | solution.py:27
  14.4 56.8 %collective-permute-start.1 = (bf16[256,512]{1,0:T(8,128)(2,1)S(1)}, bf16[256,512]{1,0:T(8,128)(2,1)S(1)}, u32[]{:S(2)}, u32[]{:S(2)}) collective-permute-start(bf16[256,512]{1,0:T(8,128)(2,1)S(1)} %pad_maximum_fusion.8), channel_id=1, source_target_pairs={{0,4},{1,5},{2,6},{3,7},{4,0},{5,1},{6,2},{7,3},{8,12},{9,13},{10,... | collective-permute-start | bytes 786440 | tf_op jit(solution)/shard_map/ppermute | solution.py:27
  14.6 62.3 %collective-permute-start.15 = (bf16[256,512]{1,0:T(8,128)(2,1)S(1)}, bf16[256,512]{1,0:T(8,128)(2,1)S(1)}, u32[]{:S(2)}, u32[]{:S(2)}) collective-permute-start(bf16[256,512]{1,0:T(8,128)(2,1)S(1)} %pad_maximum_fusion.10), channel_id=1, source_target_pairs={{0,4},{1,5},{2,6},{3,7},{4,0},{5,1},{6,2},{7,3},{8,12},{9,13},{10,... | collective-permute-start | bytes 786440 | tf_op jit(solution)/shard_map/ppermute | solution.py:27
  71.3 12.2 %collective-permute-start.17 = (bf16[256,512]{1,0:T(8,128)(2,1)S(1)}, bf16[256,512]{1,0:T(8,128)(2,1)S(1)}, u32[]{:S(2)}, u32[]{:S(2)}) collective-permute-start(bf16[256,512]{1,0:T(8,128)(2,1)S(1)} %pad_maximum_fusion.11), channel_id=1, source_target_pairs={{0,20},{1,21},{2,22},{3,23},{4,16},{5,17},{6,18},{7,19},{8,28},{9,... | collective-permute-start | bytes 786440 | tf_op jit(solution)/shard_map/ppermute | solution.py:27
  71.9 16.2 %collective-permute-start.26 = (bf16[256,512]{1,0:T(8,128)(2,1)S(1)}, bf16[256,512]{1,0:T(8,128)(2,1)S(1)}, u32[]{:S(2)}, u32[]{:S(2)}) collective-permute-start(bf16[256,512]{1,0:T(8,128)(2,1)S(1)} %pad_maximum_fusion.12), channel_id=1, source_target_pairs={{0,4},{1,5},{2,6},{3,7},{4,0},{5,1},{6,2},{7,3},{8,12},{9,13},{10,... | collective-permute-start | bytes 786440 | tf_op jit(solution)/shard_map/ppermute | solution.py:27
  76.9 13.0 %collective-permute-start.27 = (bf16[256,512]{1,0:T(8,128)(2,1)S(1)}, bf16[256,512]{1,0:T(8,128)(2,1)S(1)}, u32[]{:S(2)}, u32[]{:S(2)}) collective-permute-start(bf16[256,512]{1,0:T(8,128)(2,1)S(1)} %pad_maximum_fusion.13), channel_id=1, source_target_pairs={{0,16},{1,17},{2,18},{3,19},{4,20},{5,21},{6,22},{7,23},{8,24},{9,... | collective-permute-start | bytes 786440 | tf_op jit(solution)/shard_map/ppermute | solution.py:27
  80.5 22.8 %collective-permute-start.7 = (bf16[1024,512]{1,0:T(8,128)(2,1)S(1)}, bf16[1024,512]{1,0:T(8,128)(2,1)S(1)}, u32[]{:S(2)}, u32[]{:S(2)}) collective-permute-start(bf16[1024,512]{1,0:T(8,128)(2,1)S(1)} %constant_dynamic-update-slice_fusion), channel_id=1, source_target_pairs={{0,3},{1,0},{2,1},{3,2},{4,7},{5,4},{6,5},{7,6},{8,11},{9,8},{10,9... | collective-permute-start | bytes 3145736 | tf_op jit(solution)/shard_map/ppermute | solution.py:27
  88.1 27.3 %collective-permute-start.8 = (bf16[1024,512]{1,0:T(8,128)(2,1)S(1)}, bf16[1024,512]{1,0:T(8,128)(2,1)S(1)}, u32[]{:S(2)}, u32[]{:S(2)}) collective-permute-start(bf16[1024,512]{1,0:T(8,128)(2,1)S(1)} %constant_dynamic-update-slice_fusion), channel_id=1, source_target_pairs={{0,1},{1,2},{2,3},{3,0},{4,5},{5,6},{6,7},{7,4},{8,9},{9,10},{10,1... | collective-permute-start | bytes 3145736 | tf_op jit(solution)/shard_map/ppermute | solution.py:27
  89.9 48.0 %collective-permute-start.19 = (bf16[1024,512]{1,0:T(8,128)(2,1)S(1)}, bf16[1024,512]{1,0:T(8,128)(2,1)S(1)}, u32[]{:S(2)}, u32[]{:S(2)}) collective-permute-start(bf16[1024,512]{1,0:T(8,128)(2,1)S(1)} %constant_dynamic-update-slice_fusion.5), channel_id=1, source_target_pairs={{0,1},{1,2},{2,3},{3,0},{4,5},{5,6},{6,7},{7,4},{8,9},{9,10},{10,1... | collective-permute-start | bytes 3145736 | tf_op jit(solution)/shard_map/ppermute | solution.py:27
  91.5 72.9 %collective-permute-start.6 = (bf16[4,2,128,1024]{3,2,1,0:T(8,128)(2,1)S(1)}, bf16[4,2,128,1024]{3,2,1,0:T(8,128)(2,1)S(1)}, u32[]{:S(2)}, u32[]{:S(2)}) collective-permute-start(bf16[4,2,128,1024]{3,2,1,0:T(8,128)(2,1)S(1)} %collective-permute-done.5), channel_id=1, source_target_pairs={{0,8},{1,9},{2,10},{3,11},{4,12},{5,13},{6,14},{7,15},{8,0},{9,1},... | collective-permute-start | bytes 6291464 | tf_op jit(solution)/shard_map/ppermute | solution.py:27
  93.2 74.5 %collective-permute-start.4 = (bf16[4,2,128,1024]{3,2,1,0:T(8,128)(2,1)S(1)}, bf16[4,2,128,1024]{3,2,1,0:T(8,128)(2,1)S(1)}, u32[]{:S(2)}, u32[]{:S(2)}) collective-permute-start(bf16[4,2,128,1024]{3,2,1,0:T(8,128)(2,1)S(1)} %bitcast.139), channel_id=1, source_target_pairs={{0,8},{1,9},{2,10},{3,11},{4,12},{5,13},{6,14},{7,15},{8,0},{9,1},... | collective-permute-start | bytes 6291464 | tf_op jit(solution)/shard_map/ppermute | solution.py:27
  103.3 36.5 %collective-permute-start.18 = (bf16[1024,512]{1,0:T(8,128)(2,1)S(1)}, bf16[1024,512]{1,0:T(8,128)(2,1)S(1)}, u32[]{:S(2)}, u32[]{:S(2)}) collective-permute-start(bf16[1024,512]{1,0:T(8,128)(2,1)S(1)} %constant_dynamic-update-slice_fusion.5), channel_id=1, source_target_pairs={{0,3},{1,0},{2,1},{3,2},{4,7},{5,4},{6,5},{7,6},{8,11},{9,8},{10,9... | collective-permute-start | bytes 3145736 | tf_op jit(solution)/shard_map/ppermute | solution.py:27
  115.4 43.1 %collective-permute-start.30 = (bf16[1024,512]{1,0:T(8,128)(2,1)S(1)}, bf16[1024,512]{1,0:T(8,128)(2,1)S(1)}, u32[]{:S(2)}, u32[]{:S(2)}) collective-permute-start(bf16[1024,512]{1,0:T(8,128)(2,1)S(1)} %constant_dynamic-update-slice_fusion.10), channel_id=1, source_target_pairs={{0,1},{1,2},{2,3},{3,0},{4,5},{5,6},{6,7},{7,4},{8,9},{9,10},{10,1... | collective-permute-start | bytes 3145736 | tf_op jit(solution)/shard_map/ppermute | solution.py:27
  137.9 26.1 %collective-permute-start.29 = (bf16[1024,512]{1,0:T(8,128)(2,1)S(1)}, bf16[1024,512]{1,0:T(8,128)(2,1)S(1)}, u32[]{:S(2)}, u32[]{:S(2)}) collective-permute-start(bf16[1024,512]{1,0:T(8,128)(2,1)S(1)} %constant_dynamic-update-slice_fusion.10), channel_id=1, source_target_pairs={{0,3},{1,0},{2,1},{3,2},{4,7},{5,4},{6,5},{7,6},{8,11},{9,8},{10,9... | collective-permute-start | bytes 3145736 | tf_op jit(solution)/shard_map/ppermute | solution.py:27
  139.8 35.6 %collective-permute-start.10 = (bf16[512,512]{1,0:T(8,128)(2,1)S(1)}, bf16[512,512]{1,0:T(8,128)(2,1)S(1)}, u32[]{:S(2)}, u32[]{:S(2)}) collective-permute-start(bf16[512,512]{1,0:T(8,128)(2,1)S(1)} %slice.203), channel_id=1, source_target_pairs={{0,3},{1,0},{2,1},{3,2},{4,7},{5,4},{6,5},{7,6},{8,11},{9,8},{10,9... | collective-permute-start | bytes 1572872 | tf_op jit(solution)/shard_map/ppermute | solution.py:27
  158.5 20.1 %collective-permute-start.9 = (bf16[512,512]{1,0:T(8,128)(2,1)S(1)}, bf16[512,512]{1,0:T(8,128)(2,1)S(1)}, u32[]{:S(2)}, u32[]{:S(2)}) collective-permute-start(bf16[512,512]{1,0:T(8,128)(2,1)S(1)} %slice.202), channel_id=1, source_target_pairs={{0,1},{1,2},{2,3},{3,0},{4,5},{5,6},{6,7},{7,4},{8,9},{9,10},{10,1... | collective-permute-start | bytes 1572872 | tf_op jit(solution)/shard_map/ppermute | solution.py:27
  164.0 21.9 %collective-permute-start.20 = (bf16[512,512]{1,0:T(8,128)(2,1)S(1)}, bf16[512,512]{1,0:T(8,128)(2,1)S(1)}, u32[]{:S(2)}, u32[]{:S(2)}) collective-permute-start(bf16[512,512]{1,0:T(8,128)(2,1)S(1)} %slice.215), channel_id=1, source_target_pairs={{0,1},{1,2},{2,3},{3,0},{4,5},{5,6},{6,7},{7,4},{8,9},{9,10},{10,1... | collective-permute-start | bytes 1572872 | tf_op jit(solution)/shard_map/ppermute | solution.py:27
  164.4 22.3 %collective-permute-start.21 = (bf16[512,512]{1,0:T(8,128)(2,1)S(1)}, bf16[512,512]{1,0:T(8,128)(2,1)S(1)}, u32[]{:S(2)}, u32[]{:S(2)}) collective-permute-start(bf16[512,512]{1,0:T(8,128)(2,1)S(1)} %slice.216), channel_id=1, source_target_pairs={{0,3},{1,0},{2,1},{3,2},{4,7},{5,4},{6,5},{7,6},{8,11},{9,8},{10,9... | collective-permute-start | bytes 1572872 | tf_op jit(solution)/shard_map/ppermute | solution.py:27
  167.7 26.6 %collective-permute-start.31 = (bf16[512,512]{1,0:T(8,128)(2,1)S(1)}, bf16[512,512]{1,0:T(8,128)(2,1)S(1)}, u32[]{:S(2)}, u32[]{:S(2)}) collective-permute-start(bf16[512,512]{1,0:T(8,128)(2,1)S(1)} %slice.228), channel_id=1, source_target_pairs={{0,1},{1,2},{2,3},{3,0},{4,5},{5,6},{6,7},{7,4},{8,9},{9,10},{10,1... | collective-permute-start | bytes 1572872 | tf_op jit(solution)/shard_map/ppermute | solution.py:27
  175.4 19.8 %collective-permute-start.32 = (bf16[512,512]{1,0:T(8,128)(2,1)S(1)}, bf16[512,512]{1,0:T(8,128)(2,1)S(1)}, u32[]{:S(2)}, u32[]{:S(2)}) collective-permute-start(bf16[512,512]{1,0:T(8,128)(2,1)S(1)} %slice.229), channel_id=1, source_target_pairs={{0,3},{1,0},{2,1},{3,2},{4,7},{5,4},{6,5},{7,6},{8,11},{9,8},{10,9... | collective-permute-start | bytes 1572872 | tf_op jit(solution)/shard_map/ppermute | solution.py:27
  180.2 18.9 %collective-permute-start.11 = (f32[128,512]{1,0:T(8,128)S(1)}, f32[128,512]{1,0:T(8,128)S(1)}, u32[]{:S(2)}, u32[]{:S(2)}) collective-permute-start(f32[128,512]{1,0:T(8,128)S(1)} %get-tuple-element.11), channel_id=1, source_target_pairs={{0,32},{1,33},{2,34},{3,35},{4,36},{5,37},{6,38},{7,39},{8,40},{9,... | collective-permute-start | bytes 786440 | tf_op jit(solution)/shard_map/ppermute | solution.py:27
  185.8 13.2 %collective-permute-start.13 = (f32[128,512]{1,0:T(8,128)S(1)}, f32[128,512]{1,0:T(8,128)S(1)}, u32[]{:S(2)}, u32[]{:S(2)}) collective-permute-start(f32[128,512]{1,0:T(8,128)S(1)} %get-tuple-element.12), channel_id=1, source_target_pairs={{0,96},{1,97},{2,98},{3,99},{4,100},{5,101},{6,102},{7,103},{8,104... | collective-permute-start | bytes 786440 | tf_op jit(solution)/shard_map/ppermute | solution.py:27
  188.1 14.5 %collective-permute-start.22 = (f32[128,512]{1,0:T(8,128)S(1)}, f32[128,512]{1,0:T(8,128)S(1)}, u32[]{:S(2)}, u32[]{:S(2)}) collective-permute-start(f32[128,512]{1,0:T(8,128)S(1)} %get-tuple-element.17), channel_id=1, source_target_pairs={{0,32},{1,33},{2,34},{3,35},{4,36},{5,37},{6,38},{7,39},{8,40},{9,... | collective-permute-start | bytes 786440 | tf_op jit(solution)/shard_map/ppermute | solution.py:27
  199.1 10.8 %collective-permute-start.35 = (f32[128,512]{1,0:T(8,128)S(1)}, f32[128,512]{1,0:T(8,128)S(1)}, u32[]{:S(2)}, u32[]{:S(2)}) collective-permute-start(f32[128,512]{1,0:T(8,128)S(1)} %get-tuple-element.24), channel_id=1, source_target_pairs={{0,96},{1,97},{2,98},{3,99},{4,100},{5,101},{6,102},{7,103},{8,104... | collective-permute-start | bytes 786440 | tf_op jit(solution)/shard_map/ppermute | solution.py:27
  199.2 17.9 %collective-permute-start.12 = (f32[128,1024]{1,0:T(8,128)S(1)}, f32[128,1024]{1,0:T(8,128)S(1)}, u32[]{:S(2)}, u32[]{:S(2)}) collective-permute-start(f32[128,1024]{1,0:T(8,128)S(1)} %pad_maximum_fusion.2), channel_id=1, source_target_pairs={{0,32},{1,33},{2,34},{3,35},{4,36},{5,37},{6,38},{7,39},{8,40},{9,... | collective-permute-start | bytes 1572872 | tf_op jit(solution)/shard_map/ppermute | solution.py:27
  202.6 18.5 %collective-permute-start.14 = (f32[128,1024]{1,0:T(8,128)S(1)}, f32[128,1024]{1,0:T(8,128)S(1)}, u32[]{:S(2)}, u32[]{:S(2)}) collective-permute-start(f32[128,1024]{1,0:T(8,128)S(1)} %pad_maximum_fusion.3), channel_id=1, source_target_pairs={{0,96},{1,97},{2,98},{3,99},{4,100},{5,101},{6,102},{7,103},{8,104... | collective-permute-start | bytes 1572872 | tf_op jit(solution)/shard_map/ppermute | solution.py:27
  204.4 24.0 %collective-permute-start.23 = (f32[128,1024]{1,0:T(8,128)S(1)}, f32[128,1024]{1,0:T(8,128)S(1)}, u32[]{:S(2)}, u32[]{:S(2)}) collective-permute-start(f32[128,1024]{1,0:T(8,128)S(1)} %pad_maximum_fusion.4), channel_id=1, source_target_pairs={{0,32},{1,33},{2,34},{3,35},{4,36},{5,37},{6,38},{7,39},{8,40},{9,... | collective-permute-start | bytes 1572872 | tf_op jit(solution)/shard_map/ppermute | solution.py:27
  206.1 26.2 %collective-permute-start.25 = (f32[128,1024]{1,0:T(8,128)S(1)}, f32[128,1024]{1,0:T(8,128)S(1)}, u32[]{:S(2)}, u32[]{:S(2)}) collective-permute-start(f32[128,1024]{1,0:T(8,128)S(1)} %pad_maximum_fusion.5), channel_id=1, source_target_pairs={{0,96},{1,97},{2,98},{3,99},{4,100},{5,101},{6,102},{7,103},{8,104... | collective-permute-start | bytes 1572872 | tf_op jit(solution)/shard_map/ppermute | solution.py:27
  210.0 25.7 %collective-permute-start.34 = (f32[128,1024]{1,0:T(8,128)S(1)}, f32[128,1024]{1,0:T(8,128)S(1)}, u32[]{:S(2)}, u32[]{:S(2)}) collective-permute-start(f32[128,1024]{1,0:T(8,128)S(1)} %pad_maximum_fusion.6), channel_id=1, source_target_pairs={{0,32},{1,33},{2,34},{3,35},{4,36},{5,37},{6,38},{7,39},{8,40},{9,... | collective-permute-start | bytes 1572872 | tf_op jit(solution)/shard_map/ppermute | solution.py:27
  217.1 24.1 %collective-permute-start.36 = (f32[128,1024]{1,0:T(8,128)S(1)}, f32[128,1024]{1,0:T(8,128)S(1)}, u32[]{:S(2)}, u32[]{:S(2)}) collective-permute-start(f32[128,1024]{1,0:T(8,128)S(1)} %pad_maximum_fusion.7), channel_id=1, source_target_pairs={{0,96},{1,97},{2,98},{3,99},{4,100},{5,101},{6,102},{7,103},{8,104... | collective-permute-start | bytes 1572872 | tf_op jit(solution)/shard_map/ppermute | solution.py:27
  (8 other events, 49.9 us)

commit v2 on v1

--- a/solution.py
+++ b/solution.py
@@ -50,7 +50,8 @@
             pl.BlockSpec(memory_space=pltpu.VMEM),
         ],
         out_specs=pl.BlockSpec(memory_space=pltpu.VMEM),
-        compiler_params=pltpu.CompilerParams(vmem_limit_bytes=32 * 1024 * 1024),
+        compiler_params=pltpu.CompilerParams(vmem_limit_bytes=8 * 1024 * 1024),
+        cost_estimate=pl.CostEstimate(flops=0, bytes_accessed=8 * 1024 * 1024, transcendentals=0),
     )(where, mant, jnp.exp2(exponent.astype(jnp.float32)))
 
 
@@ -73,7 +74,8 @@
             ],
             out_specs=pl.BlockSpec((1, BLOCK, width), lambda i, order: (i, 0, 0)),
         ),
-        compiler_params=pltpu.CompilerParams(vmem_limit_bytes=32 * 1024 * 1024),
+        compiler_params=pltpu.CompilerParams(vmem_limit_bytes=8 * 1024 * 1024),
+        cost_estimate=pl.CostEstimate(flops=0, bytes_accessed=16 * 1024 * 1024, transcendentals=0),
     )(order, mant, scale)
 
 
@@ -81,6 +83,13 @@
     return lax.dot_general(
         left, right, (((0,), (0,)), ((), ())), preferred_element_type=jnp.float32
     )
+
+
+Z_PAIRS = [[base, base + 2] for base in range(16) if base % 4 < 2]
+
+
+def tied(values, *others):
+    return lax.optimization_barrier((*values, *others))[: len(values)]
 
 
 def body(act_mant, act_exp, grad_mant, grad_exp):
@@ -92,42 +101,82 @@
     order = jnp.stack(
         [(z_hi ^ flip) * 4 + (y + step) % 4 for step in range(4) for flip in range(2)]
     ).astype(jnp.int32)
+    other = send(act[1], core=1)
+    (grad_mant,) = tied((grad_mant,), act)
     own_grad = widen_grad(grad_mant, grad_exp, order).reshape(4, 2, BLOCK, -1)
+    width = own_grad.shape[-1]
+    half = width // 2
 
-    other = send(act[1], core=1)
-    grad_c = send(own_grad, core=1)
-    grad_z = send(own_grad, z=1)
-    grad_zc = send(grad_z, core=1)
-    grads = jnp.stack(
-        [
-            jnp.stack([own_grad, grad_c], axis=2),
-            jnp.stack([grad_z, grad_zc], axis=2),
-        ],
-        axis=1,
-    ).reshape(4, 8 * BLOCK, -1)
+    def halves(k):
+        return [jnp.concatenate([act[0, flip, k], other[flip, k]], axis=0) for flip in range(2)]
 
-    width = grads.shape[-1]
-    half = width // 2
-    rows = []
-    for k in range(PARTS):
-        here, there = (
-            jnp.concatenate([act[0, flip, k], other[flip, k]], axis=0) for flip in range(2)
-        )
-        piece = jnp.concatenate(
-            [here, send(here, z=2), send(there, z=1), send(there, z=3)], axis=0
-        )
-        mid = piece.shape[0] // 2
-        behind = send(piece, y=1)
-        ahead = send(piece, y=3)
-        far = jnp.concatenate([send(behind[:mid], y=1), send(ahead[mid:], y=3)], axis=0)
-        total = contract(piece, grads[0]) + contract(ahead, grads[1])
-        total = total + contract(behind, grads[3]) + contract(far, grads[2])
-        total = total.reshape(4, BLOCK, width)
-        first = send(total[2, :, :half], x=1)
-        second = send(total[2, :, half:], x=3)
+    def along_z(here, there):
+        return [here, send(here, z=2), send(there, z=1), send(there, z=3)]
+
+    def around_y(piece):
+        return send(piece, y=1), send(piece, y=3)
+
+    def onward_y(behind, ahead):
+        mid = behind.shape[0] // 2
+        return send(behind[:mid], y=1), send(ahead[mid:], y=3)
+
+    def partial(piece, ahead, behind):
+        return contract(piece, grads[0]) + contract(ahead, grads[1]) + contract(behind, grads[3])
+
+    def finish(total, far):
+        return (total + contract(jnp.concatenate(far, axis=0), grads[2])).reshape(4, BLOCK, width)
+
+    def first_x(total):
+        return send(total[2, :, :half], x=1), send(total[2, :, half:], x=3)
+
+    def second_x(total, first, second):
         to_next = jnp.concatenate([total[1, :, :half] + first, total[1, :, half:]], axis=1)
         to_last = jnp.concatenate([total[3, :, :half], total[3, :, half:] + second], axis=1)
-        rows.append(total[0] + send(to_next, x=1) + send(to_last, x=3))
+        return send(to_next, x=1), send(to_last, x=3)
+
+    half0, half1, half2 = halves(0), halves(1), halves(2)
+    z0 = along_z(*half0)
+    (for_core,) = tied((own_grad,), other)
+    grad_c = send(for_core, core=1)
+    piece0 = jnp.concatenate(z0, axis=0)
+    z1 = along_z(*tied(half1, piece0))
+    behind0, ahead0 = around_y(piece0)
+    piece1 = jnp.concatenate(z1, axis=0)
+    (for_z,) = tied((own_grad,), piece1)
+    grad_z = send(for_z, z=1)
+
+    behind0, ahead0, piece1 = tied((behind0, ahead0, piece1), grad_c)
+    far0 = onward_y(behind0, ahead0)
+    behind1, ahead1 = around_y(piece1)
+    z2 = along_z(*tied(half2, *far0))
+    piece2 = jnp.concatenate(z2, axis=0)
+    behind1, ahead1, piece2 = tied((behind1, ahead1, piece2))
+    far1 = onward_y(behind1, ahead1)
+    behind2, ahead2 = around_y(piece2)
+
+    (for_zc,) = tied((grad_z,), behind1)
+    grad_zc = send(for_zc, core=1)
+    grads = jnp.stack(
+        [jnp.stack([own_grad, grad_c], axis=2), jnp.stack([grad_z, grad_zc], axis=2)], axis=1
+    ).reshape(4, 8 * BLOCK, width)
+
+    total0 = finish(partial(piece0, ahead0, behind0), far0)
+    total0, *far1 = tied((total0, *far1))
+    x0 = first_x(total0)
+    part1 = partial(piece1, ahead1, behind1)
+    behind2, ahead2, part1, *x0 = tied((behind2, ahead2, part1, *x0))
+    far2 = onward_y(behind2, ahead2)
+    w0 = second_x(total0, *x0)
+    total1 = finish(part1, far1)
+    part2 = partial(piece2, ahead2, behind2)
+    x1 = first_x(total1)
+    part2, total1, *w0 = tied((part2, total1, *w0))
+    part2, *far2 = tied((part2, *far2), *x1)
+    total2 = finish(part2, far2)
+    w1 = second_x(total1, *x1)
+    x2 = first_x(total2)
+    w2 = second_x(total2, *x2)
+    rows = [total[0] + w[0] + w[1] for total, w in ((total0, w0), (total1, w1), (total2, w2))]
     return jnp.concatenate(rows, axis=0)
 
 

time: 243 us -> 208 us (0.86)
  waiting for transfers between devices: 164 us -> 128 us
    ppermute x37, waiting for transfers between devices: 164 us -> 128 us  [send(): return lax.ppermute(value, AXES, pairs)]
  transfers between devices with their start and end apart: 37 -> 37, of which waited for: 21 -> 21; matrix products, arithmetic and copies ran while one was open for 8% -> 8% of each run, Pallas kernels for 0% -> 1%
where the time goes in v2:
time: 208 us; the launch traced here: 207 us
  waiting for transfers between devices  128 us (62%)
  starting transfers between devices  50.8 us (24%)
  matrix products  15.4 us (7%)
  local copies, waits for them, and re-layouts  5.06 us (2%)
  other arithmetic  5 us (2%)
  Pallas kernels  2.56 us (1%)
    ppermute x37, waiting for transfers between devices, send(): return lax.ppermute(value, AXES, pairs)  128 us
    ppermute x37, starting transfers between devices, send(): return lax.ppermute(value, AXES, pairs)  50.8 us
    dot_general x12, matrix products, contract(): lax.dot_general(left, right, (((0,), (0,)), ((), ())), preferred_element_...  15.4 us
    unnamed x13, local copies, waits for them, and re-layouts  4.2 us
  transfers between devices with their start and end apart: 37, of which 21 were waited for; matrix products, arithmetic and copies ran while one was open for 8% of the time, Pallas kernels for 1%

profile of v2, /device:TPU:6, one launch (start us, length us, event | category | flops | bytes accessed | tf_op | source)
XLA Modules:
  0.0 207.0 jit_solution(5528132255881350412)
XLA Ops:
  1.0 1.9 copy-done.1
  4.8 2.2 %copy-done = s32[1024,1024]{1,0:T(8,128)S(1)} copy-done((s32[1024,1024]{1,0:T(8,128)S(1)}, s32[1024,1024]{1,0:T(8,128)}, u32[]{:S(2)}) %copy-start) | copy-done | bytes 4194328
  8.2 2.0 collective-permute-start.2
  10.2 2.5 %collective-permute-start.3 = (bf16[256,512]{1,0:T(8,128)(2,1)S(1)}, bf16[256,512]{1,0:T(8,128)(2,1)S(1)}, u32[]{:S(2)}, u32[]{:S(2)}) collective-permute-start(bf16[256,512]{1,0:T(8,128)(2,1)S(1)} %pad_maximum_fusion.10), channel_id=1, source_target_pairs={{0,20},{1,21},{2,22},{3,23},{4,16},{5,17},{6,18},{7,19},{8,28},{9,... | collective-permute-start | bytes 786440 | tf_op jit(solution)/shard_map/ppermute | solution.py:27
  14.0 12.1 %collective-permute-done.1 = bf16[256,512]{1,0:T(8,128)(2,1)S(1)} collective-permute-done((bf16[256,512]{1,0:T(8,128)(2,1)S(1)}, bf16[256,512]{1,0:T(8,128)(2,1)S(1)}, u32[]{:S(2)}, u32[]{:S(2)}) %collective-permute-start.1) | collective-permute-done | bytes 262176 | tf_op jit(solution)/shard_map/ppermute | solution.py:27
  26.1 1.8 collective-permute-start.5
  30.3 3.1 %collective-permute-start.10 = (bf16[1024,512]{1,0:T(8,128)(2,1)S(1)}, bf16[1024,512]{1,0:T(8,128)(2,1)S(1)}, u32[]{:S(2)}, u32[]{:S(2)}) collective-permute-start(bf16[1024,512]{1,0:T(8,128)(2,1)S(1)} %constant_dynamic-update-slice_fusion), channel_id=1, source_target_pairs={{0,3},{1,0},{2,1},{3,2},{4,7},{5,4},{6,5},{7,6},{8,11},{9,8},{10,9... | collective-permute-start | bytes 3145736 | tf_op jit(solution)/shard_map/ppermute | solution.py:27
  33.4 3.6 %collective-permute-done.5 = bf16[256,512]{1,0:T(8,128)(2,1)S(1)} collective-permute-done((bf16[256,512]{1,0:T(8,128)(2,1)S(1)}, bf16[256,512]{1,0:T(8,128)(2,1)S(1)}, u32[]{:S(2)}, u32[]{:S(2)}) %collective-permute-start.5) | collective-permute-done | bytes 262176 | tf_op jit(solution)/shard_map/ppermute | solution.py:27
  41.3 13.5 %collective-permute-done.10 = bf16[1024,512]{1,0:T(8,128)(2,1)S(1)} collective-permute-done((bf16[1024,512]{1,0:T(8,128)(2,1)S(1)}, bf16[1024,512]{1,0:T(8,128)(2,1)S(1)}, u32[]{:S(2)}, u32[]{:S(2)}) %collective-permute-start.10) | collective-permute-done | bytes 1048608 | tf_op jit(solution)/shard_map/ppermute | solution.py:27
  54.8 5.9 %collective-permute-done.9 = bf16[1024,512]{1,0:T(8,128)(2,1)S(1)} collective-permute-done((bf16[1024,512]{1,0:T(8,128)(2,1)S(1)}, bf16[1024,512]{1,0:T(8,128)(2,1)S(1)}, u32[]{:S(2)}, u32[]{:S(2)}) %collective-permute-start.9) | collective-permute-done | bytes 1048608 | tf_op jit(solution)/shard_map/ppermute | solution.py:27
  61.9 2.3 %collective-permute-start.14 = (bf16[512,512]{1,0:T(8,128)(2,1)S(1)}, bf16[512,512]{1,0:T(8,128)(2,1)S(1)}, u32[]{:S(2)}, u32[]{:S(2)}) collective-permute-start(bf16[512,512]{1,0:T(8,128)(2,1)S(1)} %slice.159), channel_id=1, source_target_pairs={{0,3},{1,0},{2,1},{3,2},{4,7},{5,4},{6,5},{7,6},{8,11},{9,8},{10,9... | collective-permute-start | bytes 1572872 | tf_op jit(solution)/shard_map/ppermute | solution.py:27
  64.1 3.2 %collective-permute-start.12 = (bf16[1024,512]{1,0:T(8,128)(2,1)S(1)}, bf16[1024,512]{1,0:T(8,128)(2,1)S(1)}, u32[]{:S(2)}, u32[]{:S(2)}) collective-permute-start(bf16[1024,512]{1,0:T(8,128)(2,1)S(1)} %constant_dynamic-update-slice_fusion.5), channel_id=1, source_target_pairs={{0,3},{1,0},{2,1},{3,2},{4,7},{5,4},{6,5},{7,6},{8,11},{9,8},{10,9... | collective-permute-start | bytes 3145736 | tf_op jit(solution)/shard_map/ppermute | solution.py:27
  67.4 9.5 %collective-permute-done.13 = bf16[512,512]{1,0:T(8,128)(2,1)S(1)} collective-permute-done((bf16[512,512]{1,0:T(8,128)(2,1)S(1)}, bf16[512,512]{1,0:T(8,128)(2,1)S(1)}, u32[]{:S(2)}, u32[]{:S(2)}) %collective-permute-start.13) | collective-permute-done | bytes 524320 | tf_op jit(solution)/shard_map/ppermute | solution.py:27
  79.5 16.8 %collective-permute-done.15 = bf16[256,512]{1,0:T(8,128)(2,1)S(1)} collective-permute-done((bf16[256,512]{1,0:T(8,128)(2,1)S(1)}, bf16[256,512]{1,0:T(8,128)(2,1)S(1)}, u32[]{:S(2)}, u32[]{:S(2)}) %collective-permute-start.15) | collective-permute-done | bytes 262176 | tf_op jit(solution)/shard_map/ppermute | solution.py:27
  96.3 1.7 collective-permute-start.17
  98.1 2.0 collective-permute-done.16
  100.1 3.9 %collective-permute-done.17 = bf16[256,512]{1,0:T(8,128)(2,1)S(1)} collective-permute-done((bf16[256,512]{1,0:T(8,128)(2,1)S(1)}, bf16[256,512]{1,0:T(8,128)(2,1)S(1)}, u32[]{:S(2)}, u32[]{:S(2)}) %collective-permute-start.17) | collective-permute-done | bytes 262176 | tf_op jit(solution)/shard_map/ppermute | solution.py:27
  104.2 1.6 collective-permute-start.21
  105.9 1.7 collective-permute-start.22
  107.9 3.1 %collective-permute-start.20 = (bf16[512,512]{1,0:T(8,128)(2,1)S(1)}, bf16[512,512]{1,0:T(8,128)(2,1)S(1)}, u32[]{:S(2)}, u32[]{:S(2)}) collective-permute-start(bf16[512,512]{1,0:T(8,128)(2,1)S(1)} %slice.165), channel_id=1, source_target_pairs={{0,3},{1,0},{2,1},{3,2},{4,7},{5,4},{6,5},{7,6},{8,11},{9,8},{10,9... | collective-permute-start | bytes 1572872 | tf_op jit(solution)/shard_map/ppermute | solution.py:27
  121.2 21.1 %collective-permute-done.19 = bf16[512,512]{1,0:T(8,128)(2,1)S(1)} collective-permute-done((bf16[512,512]{1,0:T(8,128)(2,1)S(1)}, bf16[512,512]{1,0:T(8,128)(2,1)S(1)}, u32[]{:S(2)}, u32[]{:S(2)}) %collective-permute-start.19) | collective-permute-done | bytes 524320 | tf_op jit(solution)/shard_map/ppermute | solution.py:27
  147.2 3.3 %collective-permute-done.23 = f32[128,512]{1,0:T(8,128)S(1)} collective-permute-done((f32[128,512]{1,0:T(8,128)S(1)}, f32[128,512]{1,0:T(8,128)S(1)}, u32[]{:S(2)}, u32[]{:S(2)}) %collective-permute-start.23) | collective-permute-done | bytes 262176 | tf_op jit(solution)/shard_map/ppermute | solution.py:27
  152.5 3.0 %collective-permute-start.25 = (f32[128,1024]{1,0:T(8,128)S(1)}, f32[128,1024]{1,0:T(8,128)S(1)}, u32[]{:S(2)}, u32[]{:S(2)}) collective-permute-start(f32[128,1024]{1,0:T(8,128)S(1)} %pad_maximum_fusion.3), channel_id=1, source_target_pairs={{0,32},{1,33},{2,34},{3,35},{4,36},{5,37},{6,38},{7,39},{8,40},{9,... | collective-permute-start | bytes 1572872 | tf_op jit(solution)/shard_map/ppermute | solution.py:27
  156.0 2.0 collective-permute-start.29
  160.8 7.4 %collective-permute-done.26 = f32[128,1024]{1,0:T(8,128)S(1)} collective-permute-done((f32[128,1024]{1,0:T(8,128)S(1)}, f32[128,1024]{1,0:T(8,128)S(1)}, u32[]{:S(2)}, u32[]{:S(2)}) %collective-permute-start.26) | collective-permute-done | bytes 524320 | tf_op jit(solution)/shard_map/ppermute | solution.py:27
  168.2 2.8 %collective-permute-start.32 = (bf16[512,512]{1,0:T(8,128)(2,1)S(1)}, bf16[512,512]{1,0:T(8,128)(2,1)S(1)}, u32[]{:S(2)}, u32[]{:S(2)}) collective-permute-start(bf16[512,512]{1,0:T(8,128)(2,1)S(1)} %slice.181), channel_id=1, source_target_pairs={{0,3},{1,0},{2,1},{3,2},{4,7},{5,4},{6,5},{7,6},{8,11},{9,8},{10,9... | collective-permute-start | bytes 1572872 | tf_op jit(solution)/shard_map/ppermute | solution.py:27
  172.3 5.4 %collective-permute-done.32 = bf16[512,512]{1,0:T(8,128)(2,1)S(1)} collective-permute-done((bf16[512,512]{1,0:T(8,128)(2,1)S(1)}, bf16[512,512]{1,0:T(8,128)(2,1)S(1)}, u32[]{:S(2)}, u32[]{:S(2)}) %collective-permute-start.32) | collective-permute-done | bytes 524320 | tf_op jit(solution)/shard_map/ppermute | solution.py:27
  179.5 2.0 collective-permute-start.35
  183.9 4.8 %collective-permute-done.33 = f32[128,512]{1,0:T(8,128)S(1)} collective-permute-done((f32[128,512]{1,0:T(8,128)S(1)}, f32[128,512]{1,0:T(8,128)S(1)}, u32[]{:S(2)}, u32[]{:S(2)}) %collective-permute-start.33) | collective-permute-done | bytes 262176 | tf_op jit(solution)/shard_map/ppermute | solution.py:27
  190.3 2.1 %collective-permute-start.36 = (f32[128,1024]{1,0:T(8,128)S(1)}, f32[128,1024]{1,0:T(8,128)S(1)}, u32[]{:S(2)}, u32[]{:S(2)}) collective-permute-start(f32[128,1024]{1,0:T(8,128)S(1)} %pad_maximum_fusion.8), channel_id=1, source_target_pairs={{0,96},{1,97},{2,98},{3,99},{4,100},{5,101},{6,102},{7,103},{8,104... | collective-permute-start | bytes 1572872 | tf_op jit(solution)/shard_map/ppermute | solution.py:27
  192.5 6.0 %collective-permute-done.28 = f32[128,1024]{1,0:T(8,128)S(1)} collective-permute-done((f32[128,1024]{1,0:T(8,128)S(1)}, f32[128,1024]{1,0:T(8,128)S(1)}, u32[]{:S(2)}, u32[]{:S(2)}) %collective-permute-start.28) | collective-permute-done | bytes 524320 | tf_op jit(solution)/shard_map/ppermute | solution.py:27
  200.1 4.0 %collective-permute-done.34 = f32[128,1024]{1,0:T(8,128)S(1)} collective-permute-done((f32[128,1024]{1,0:T(8,128)S(1)}, f32[128,1024]{1,0:T(8,128)S(1)}, u32[]{:S(2)}, u32[]{:S(2)}) %collective-permute-start.34) | collective-permute-done | bytes 524320 | tf_op jit(solution)/shard_map/ppermute | solution.py:27
  (113 shorter events, 48.2 us)
Async XLA Ops:
  8.2 17.8 %collective-permute-start.2 = (bf16[256,512]{1,0:T(8,128)(2,1)S(1)}, bf16[256,512]{1,0:T(8,128)(2,1)S(1)}, u32[]{:S(2)}, u32[]{:S(2)}) collective-permute-start(bf16[256,512]{1,0:T(8,128)(2,1)S(1)} %pad_maximum_fusion.10), channel_id=1, source_target_pairs={{0,16},{1,17},{2,18},{3,19},{4,20},{5,21},{6,22},{7,23},{8,24},{9,... | collective-permute-start | bytes 786440 | tf_op jit(solution)/shard_map/ppermute | solution.py:27
  10.2 15.9 %collective-permute-start.3 = (bf16[256,512]{1,0:T(8,128)(2,1)S(1)}, bf16[256,512]{1,0:T(8,128)(2,1)S(1)}, u32[]{:S(2)}, u32[]{:S(2)}) collective-permute-start(bf16[256,512]{1,0:T(8,128)(2,1)S(1)} %pad_maximum_fusion.10), channel_id=1, source_target_pairs={{0,20},{1,21},{2,22},{3,23},{4,16},{5,17},{6,18},{7,19},{8,28},{9,... | collective-permute-start | bytes 786440 | tf_op jit(solution)/shard_map/ppermute | solution.py:27
  12.8 13.3 %collective-permute-start.1 = (bf16[256,512]{1,0:T(8,128)(2,1)S(1)}, bf16[256,512]{1,0:T(8,128)(2,1)S(1)}, u32[]{:S(2)}, u32[]{:S(2)}) collective-permute-start(bf16[256,512]{1,0:T(8,128)(2,1)S(1)} %pad_maximum_fusion.9), channel_id=1, source_target_pairs={{0,4},{1,5},{2,6},{3,7},{4,0},{5,1},{6,2},{7,3},{8,12},{9,13},{10,... | collective-permute-start | bytes 786440 | tf_op jit(solution)/shard_map/ppermute | solution.py:27
  13.9 46.8 %collective-permute-start.4 = (bf16[4,2,128,1024]{3,2,1,0:T(8,128)(2,1)S(1)}, bf16[4,2,128,1024]{3,2,1,0:T(8,128)(2,1)S(1)}, u32[]{:S(2)}, u32[]{:S(2)}) collective-permute-start(bf16[4,2,128,1024]{3,2,1,0:T(8,128)(2,1)S(1)} %bitcast.130), channel_id=1, source_target_pairs={{0,8},{1,9},{2,10},{3,11},{4,12},{5,13},{6,14},{7,15},{8,0},{9,1},... | collective-permute-start | bytes 6291464 | tf_op jit(solution)/shard_map/ppermute | solution.py:27
  26.1 10.8 %collective-permute-start.5 = (bf16[256,512]{1,0:T(8,128)(2,1)S(1)}, bf16[256,512]{1,0:T(8,128)(2,1)S(1)}, u32[]{:S(2)}, u32[]{:S(2)}) collective-permute-start(bf16[256,512]{1,0:T(8,128)(2,1)S(1)} %get-tuple-element.36), channel_id=1, source_target_pairs={{0,4},{1,5},{2,6},{3,7},{4,0},{5,1},{6,2},{7,3},{8,12},{9,13},{10,... | collective-permute-start | bytes 786440 | tf_op jit(solution)/shard_map/ppermute | solution.py:27
  27.9 12.2 %collective-permute-start.6 = (bf16[256,512]{1,0:T(8,128)(2,1)S(1)}, bf16[256,512]{1,0:T(8,128)(2,1)S(1)}, u32[]{:S(2)}, u32[]{:S(2)}) collective-permute-start(bf16[256,512]{1,0:T(8,128)(2,1)S(1)} %get-tuple-element.37), channel_id=1, source_target_pairs={{0,16},{1,17},{2,18},{3,19},{4,20},{5,21},{6,22},{7,23},{8,24},{9,... | collective-permute-start | bytes 786440 | tf_op jit(solution)/shard_map/ppermute | solution.py:27
  28.9 12.3 %collective-permute-start.7 = (bf16[256,512]{1,0:T(8,128)(2,1)S(1)}, bf16[256,512]{1,0:T(8,128)(2,1)S(1)}, u32[]{:S(2)}, u32[]{:S(2)}) collective-permute-start(bf16[256,512]{1,0:T(8,128)(2,1)S(1)} %get-tuple-element.37), channel_id=1, source_target_pairs={{0,20},{1,21},{2,22},{3,23},{4,16},{5,17},{6,18},{7,19},{8,28},{9,... | collective-permute-start | bytes 786440 | tf_op jit(solution)/shard_map/ppermute | solution.py:27
  30.3 24.5 %collective-permute-start.10 = (bf16[1024,512]{1,0:T(8,128)(2,1)S(1)}, bf16[1024,512]{1,0:T(8,128)(2,1)S(1)}, u32[]{:S(2)}, u32[]{:S(2)}) collective-permute-start(bf16[1024,512]{1,0:T(8,128)(2,1)S(1)} %constant_dynamic-update-slice_fusion), channel_id=1, source_target_pairs={{0,3},{1,0},{2,1},{3,2},{4,7},{5,4},{6,5},{7,6},{8,11},{9,8},{10,9... | collective-permute-start | bytes 3145736 | tf_op jit(solution)/shard_map/ppermute | solution.py:27
  37.0 23.7 %collective-permute-start.9 = (bf16[1024,512]{1,0:T(8,128)(2,1)S(1)}, bf16[1024,512]{1,0:T(8,128)(2,1)S(1)}, u32[]{:S(2)}, u32[]{:S(2)}) collective-permute-start(bf16[1024,512]{1,0:T(8,128)(2,1)S(1)} %constant_dynamic-update-slice_fusion), channel_id=1, source_target_pairs={{0,1},{1,2},{2,3},{3,0},{4,5},{5,6},{6,7},{7,4},{8,9},{9,10},{10,1... | collective-permute-start | bytes 3145736 | tf_op jit(solution)/shard_map/ppermute | solution.py:27
  41.2 62.9 %collective-permute-start.8 = (bf16[4,2,128,1024]{3,2,1,0:T(8,128)(2,1)S(1)}, bf16[4,2,128,1024]{3,2,1,0:T(8,128)(2,1)S(1)}, u32[]{:S(2)}, u32[]{:S(2)}) collective-permute-start(bf16[4,2,128,1024]{3,2,1,0:T(8,128)(2,1)S(1)} %bitcast.131), channel_id=1, source_target_pairs={{0,16},{1,17},{2,18},{3,19},{4,20},{5,21},{6,22},{7,23},{8,24},{9,... | collective-permute-start | bytes 6291464 | tf_op jit(solution)/shard_map/ppermute | solution.py:27
  60.7 16.1 %collective-permute-start.13 = (bf16[512,512]{1,0:T(8,128)(2,1)S(1)}, bf16[512,512]{1,0:T(8,128)(2,1)S(1)}, u32[]{:S(2)}, u32[]{:S(2)}) collective-permute-start(bf16[512,512]{1,0:T(8,128)(2,1)S(1)} %slice.158), channel_id=1, source_target_pairs={{0,1},{1,2},{2,3},{3,0},{4,5},{5,6},{6,7},{7,4},{8,9},{9,10},{10,1... | collective-permute-start | bytes 1572872 | tf_op jit(solution)/shard_map/ppermute | solution.py:27
  61.9 15.0 %collective-permute-start.14 = (bf16[512,512]{1,0:T(8,128)(2,1)S(1)}, bf16[512,512]{1,0:T(8,128)(2,1)S(1)}, u32[]{:S(2)}, u32[]{:S(2)}) collective-permute-start(bf16[512,512]{1,0:T(8,128)(2,1)S(1)} %slice.159), channel_id=1, source_target_pairs={{0,3},{1,0},{2,1},{3,2},{4,7},{5,4},{6,5},{7,6},{8,11},{9,8},{10,9... | collective-permute-start | bytes 1572872 | tf_op jit(solution)/shard_map/ppermute | solution.py:27
  64.1 39.9 %collective-permute-start.11 = (bf16[1024,512]{1,0:T(8,128)(2,1)S(1)}, bf16[1024,512]{1,0:T(8,128)(2,1)S(1)}, u32[]{:S(2)}, u32[]{:S(2)}) collective-permute-start(bf16[1024,512]{1,0:T(8,128)(2,1)S(1)} %constant_dynamic-update-slice_fusion.5), channel_id=1, source_target_pairs={{0,1},{1,2},{2,3},{3,0},{4,5},{5,6},{6,7},{7,4},{8,9},{9,10},{10,1... | collective-permute-start | bytes 3145736 | tf_op jit(solution)/shard_map/ppermute | solution.py:27
  64.1 39.9 %collective-permute-start.12 = (bf16[1024,512]{1,0:T(8,128)(2,1)S(1)}, bf16[1024,512]{1,0:T(8,128)(2,1)S(1)}, u32[]{:S(2)}, u32[]{:S(2)}) collective-permute-start(bf16[1024,512]{1,0:T(8,128)(2,1)S(1)} %constant_dynamic-update-slice_fusion.5), channel_id=1, source_target_pairs={{0,3},{1,0},{2,1},{3,2},{4,7},{5,4},{6,5},{7,6},{8,11},{9,8},{10,9... | collective-permute-start | bytes 3145736 | tf_op jit(solution)/shard_map/ppermute | solution.py:27
  76.9 19.5 %collective-permute-start.15 = (bf16[256,512]{1,0:T(8,128)(2,1)S(1)}, bf16[256,512]{1,0:T(8,128)(2,1)S(1)}, u32[]{:S(2)}, u32[]{:S(2)}) collective-permute-start(bf16[256,512]{1,0:T(8,128)(2,1)S(1)} %get-tuple-element.42), channel_id=1, source_target_pairs={{0,4},{1,5},{2,6},{3,7},{4,0},{5,1},{6,2},{7,3},{8,12},{9,13},{10,... | collective-permute-start | bytes 786440 | tf_op jit(solution)/shard_map/ppermute | solution.py:27
  78.5 21.6 %collective-permute-start.16 = (bf16[256,512]{1,0:T(8,128)(2,1)S(1)}, bf16[256,512]{1,0:T(8,128)(2,1)S(1)}, u32[]{:S(2)}, u32[]{:S(2)}) collective-permute-start(bf16[256,512]{1,0:T(8,128)(2,1)S(1)} %get-tuple-element.43), channel_id=1, source_target_pairs={{0,16},{1,17},{2,18},{3,19},{4,20},{5,21},{6,22},{7,23},{8,24},{9,... | collective-permute-start | bytes 786440 | tf_op jit(solution)/shard_map/ppermute | solution.py:27
  104.2 42.9 %collective-permute-start.21 = (bf16[1024,512]{1,0:T(8,128)(2,1)S(1)}, bf16[1024,512]{1,0:T(8,128)(2,1)S(1)}, u32[]{:S(2)}, u32[]{:S(2)}) collective-permute-start(bf16[1024,512]{1,0:T(8,128)(2,1)S(1)} %pad_maximum_fusion.2), channel_id=1, source_target_pairs={{0,1},{1,2},{2,3},{3,0},{4,5},{5,6},{6,7},{7,4},{8,9},{9,10},{10,1... | collective-permute-start | bytes 3145736 | tf_op jit(solution)/shard_map/ppermute | solution.py:27
  105.9 41.3 %collective-permute-start.22 = (bf16[1024,512]{1,0:T(8,128)(2,1)S(1)}, bf16[1024,512]{1,0:T(8,128)(2,1)S(1)}, u32[]{:S(2)}, u32[]{:S(2)}) collective-permute-start(bf16[1024,512]{1,0:T(8,128)(2,1)S(1)} %pad_maximum_fusion.2), channel_id=1, source_target_pairs={{0,3},{1,0},{2,1},{3,2},{4,7},{5,4},{6,5},{7,6},{8,11},{9,8},{10,9... | collective-permute-start | bytes 3145736 | tf_op jit(solution)/shard_map/ppermute | solution.py:27
  107.5 34.8 %collective-permute-start.19 = (bf16[512,512]{1,0:T(8,128)(2,1)S(1)}, bf16[512,512]{1,0:T(8,128)(2,1)S(1)}, u32[]{:S(2)}, u32[]{:S(2)}) collective-permute-start(bf16[512,512]{1,0:T(8,128)(2,1)S(1)} %slice.164), channel_id=1, source_target_pairs={{0,1},{1,2},{2,3},{3,0},{4,5},{5,6},{6,7},{7,4},{8,9},{9,10},{10,1... | collective-permute-start | bytes 1572872 | tf_op jit(solution)/shard_map/ppermute | solution.py:27
  107.9 34.4 %collective-permute-start.20 = (bf16[512,512]{1,0:T(8,128)(2,1)S(1)}, bf16[512,512]{1,0:T(8,128)(2,1)S(1)}, u32[]{:S(2)}, u32[]{:S(2)}) collective-permute-start(bf16[512,512]{1,0:T(8,128)(2,1)S(1)} %slice.165), channel_id=1, source_target_pairs={{0,3},{1,0},{2,1},{3,2},{4,7},{5,4},{6,5},{7,6},{8,11},{9,8},{10,9... | collective-permute-start | bytes 1572872 | tf_op jit(solution)/shard_map/ppermute | solution.py:27
  152.0 16.1 %collective-permute-start.26 = (f32[128,1024]{1,0:T(8,128)S(1)}, f32[128,1024]{1,0:T(8,128)S(1)}, u32[]{:S(2)}, u32[]{:S(2)}) collective-permute-start(f32[128,1024]{1,0:T(8,128)S(1)} %pad_maximum_fusion.4), channel_id=1, source_target_pairs={{0,96},{1,97},{2,98},{3,99},{4,100},{5,101},{6,102},{7,103},{8,104... | collective-permute-start | bytes 1572872 | tf_op jit(solution)/shard_map/ppermute | solution.py:27
  152.5 19.8 %collective-permute-start.25 = (f32[128,1024]{1,0:T(8,128)S(1)}, f32[128,1024]{1,0:T(8,128)S(1)}, u32[]{:S(2)}, u32[]{:S(2)}) collective-permute-start(f32[128,1024]{1,0:T(8,128)S(1)} %pad_maximum_fusion.3), channel_id=1, source_target_pairs={{0,32},{1,33},{2,34},{3,35},{4,36},{5,37},{6,38},{7,39},{8,40},{9,... | collective-permute-start | bytes 1572872 | tf_op jit(solution)/shard_map/ppermute | solution.py:27
  155.9 16.4 %collective-permute-start.27 = (f32[128,512]{1,0:T(8,128)S(1)}, f32[128,512]{1,0:T(8,128)S(1)}, u32[]{:S(2)}, u32[]{:S(2)}) collective-permute-start(f32[128,512]{1,0:T(8,128)S(1)} %get-tuple-element.78), channel_id=1, source_target_pairs={{0,32},{1,33},{2,34},{3,35},{4,36},{5,37},{6,38},{7,39},{8,40},{9,... | collective-permute-start | bytes 786440 | tf_op jit(solution)/shard_map/ppermute | solution.py:27
  156.0 16.3 %collective-permute-start.29 = (f32[128,512]{1,0:T(8,128)S(1)}, f32[128,512]{1,0:T(8,128)S(1)}, u32[]{:S(2)}, u32[]{:S(2)}) collective-permute-start(f32[128,512]{1,0:T(8,128)S(1)} %get-tuple-element.77), channel_id=1, source_target_pairs={{0,96},{1,97},{2,98},{3,99},{4,100},{5,101},{6,102},{7,103},{8,104... | collective-permute-start | bytes 786440 | tf_op jit(solution)/shard_map/ppermute | solution.py:27
  158.0 14.3 %collective-permute-start.31 = (bf16[512,512]{1,0:T(8,128)(2,1)S(1)}, bf16[512,512]{1,0:T(8,128)(2,1)S(1)}, u32[]{:S(2)}, u32[]{:S(2)}) collective-permute-start(bf16[512,512]{1,0:T(8,128)(2,1)S(1)} %slice.180), channel_id=1, source_target_pairs={{0,1},{1,2},{2,3},{3,0},{4,5},{5,6},{6,7},{7,4},{8,9},{9,10},{10,1... | collective-permute-start | bytes 1572872 | tf_op jit(solution)/shard_map/ppermute | solution.py:27
  168.2 9.5 %collective-permute-start.32 = (bf16[512,512]{1,0:T(8,128)(2,1)S(1)}, bf16[512,512]{1,0:T(8,128)(2,1)S(1)}, u32[]{:S(2)}, u32[]{:S(2)}) collective-permute-start(bf16[512,512]{1,0:T(8,128)(2,1)S(1)} %slice.181), channel_id=1, source_target_pairs={{0,3},{1,0},{2,1},{3,2},{4,7},{5,4},{6,5},{7,6},{8,11},{9,8},{10,9... | collective-permute-start | bytes 1572872 | tf_op jit(solution)/shard_map/ppermute | solution.py:27
  179.4 9.3 %collective-permute-start.33 = (f32[128,512]{1,0:T(8,128)S(1)}, f32[128,512]{1,0:T(8,128)S(1)}, u32[]{:S(2)}, u32[]{:S(2)}) collective-permute-start(f32[128,512]{1,0:T(8,128)S(1)} %get-tuple-element.73), channel_id=1, source_target_pairs={{0,32},{1,33},{2,34},{3,35},{4,36},{5,37},{6,38},{7,39},{8,40},{9,... | collective-permute-start | bytes 786440 | tf_op jit(solution)/shard_map/ppermute | solution.py:27
  179.5 10.5 %collective-permute-start.35 = (f32[128,512]{1,0:T(8,128)S(1)}, f32[128,512]{1,0:T(8,128)S(1)}, u32[]{:S(2)}, u32[]{:S(2)}) collective-permute-start(f32[128,512]{1,0:T(8,128)S(1)} %get-tuple-element.74), channel_id=1, source_target_pairs={{0,96},{1,97},{2,98},{3,99},{4,100},{5,101},{6,102},{7,103},{8,104... | collective-permute-start | bytes 786440 | tf_op jit(solution)/shard_map/ppermute | solution.py:27
  181.7 16.8 %collective-permute-start.28 = (f32[128,1024]{1,0:T(8,128)S(1)}, f32[128,1024]{1,0:T(8,128)S(1)}, u32[]{:S(2)}, u32[]{:S(2)}) collective-permute-start(f32[128,1024]{1,0:T(8,128)S(1)} %pad_maximum_fusion.5), channel_id=1, source_target_pairs={{0,32},{1,33},{2,34},{3,35},{4,36},{5,37},{6,38},{7,39},{8,40},{9,... | collective-permute-start | bytes 1572872 | tf_op jit(solution)/shard_map/ppermute | solution.py:27
  183.1 16.9 %collective-permute-start.30 = (f32[128,1024]{1,0:T(8,128)S(1)}, f32[128,1024]{1,0:T(8,128)S(1)}, u32[]{:S(2)}, u32[]{:S(2)}) collective-permute-start(f32[128,1024]{1,0:T(8,128)S(1)} %pad_maximum_fusion.6), channel_id=1, source_target_pairs={{0,96},{1,97},{2,98},{3,99},{4,100},{5,101},{6,102},{7,103},{8,104... | collective-permute-start | bytes 1572872 | tf_op jit(solution)/shard_map/ppermute | solution.py:27
  190.2 13.9 %collective-permute-start.34 = (f32[128,1024]{1,0:T(8,128)S(1)}, f32[128,1024]{1,0:T(8,128)S(1)}, u32[]{:S(2)}, u32[]{:S(2)}) collective-permute-start(f32[128,1024]{1,0:T(8,128)S(1)} %pad_maximum_fusion.7), channel_id=1, source_target_pairs={{0,32},{1,33},{2,34},{3,35},{4,36},{5,37},{6,38},{7,39},{8,40},{9,... | collective-permute-start | bytes 1572872 | tf_op jit(solution)/shard_map/ppermute | solution.py:27
  190.3 15.3 %collective-permute-start.36 = (f32[128,1024]{1,0:T(8,128)S(1)}, f32[128,1024]{1,0:T(8,128)S(1)}, u32[]{:S(2)}, u32[]{:S(2)}) collective-permute-start(f32[128,1024]{1,0:T(8,128)S(1)} %pad_maximum_fusion.8), channel_id=1, source_target_pairs={{0,96},{1,97},{2,98},{3,99},{4,100},{5,101},{6,102},{7,103},{8,104... | collective-permute-start | bytes 1572872 | tf_op jit(solution)/shard_map/ppermute | solution.py:27
  (8 other events, 41.1 us)

commit v3 on v1

--- a/solution.py
+++ b/solution.py
@@ -50,7 +50,8 @@
             pl.BlockSpec(memory_space=pltpu.VMEM),
         ],
         out_specs=pl.BlockSpec(memory_space=pltpu.VMEM),
-        compiler_params=pltpu.CompilerParams(vmem_limit_bytes=32 * 1024 * 1024),
+        compiler_params=pltpu.CompilerParams(vmem_limit_bytes=8 * 1024 * 1024),
+        cost_estimate=pl.CostEstimate(flops=0, bytes_accessed=8 * 1024 * 1024, transcendentals=0),
     )(where, mant, jnp.exp2(exponent.astype(jnp.float32)))
 
 
@@ -73,7 +74,8 @@
             ],
             out_specs=pl.BlockSpec((1, BLOCK, width), lambda i, order: (i, 0, 0)),
         ),
-        compiler_params=pltpu.CompilerParams(vmem_limit_bytes=32 * 1024 * 1024),
+        compiler_params=pltpu.CompilerParams(vmem_limit_bytes=8 * 1024 * 1024),
+        cost_estimate=pl.CostEstimate(flops=0, bytes_accessed=16 * 1024 * 1024, transcendentals=0),
     )(order, mant, scale)
 
 
@@ -83,6 +85,10 @@
     )
 
 
+def tied(values, *others):
+    return lax.optimization_barrier((*values, *others))[: len(values)]
+
+
 def body(act_mant, act_exp, grad_mant, grad_exp):
     dp, tensor = lax.axis_index("dp"), lax.axis_index("tensor")
     x, z_lo, core = dp // 4, (dp // 2) % 2, dp % 2
@@ -92,42 +98,98 @@
     order = jnp.stack(
         [(z_hi ^ flip) * 4 + (y + step) % 4 for step in range(4) for flip in range(2)]
     ).astype(jnp.int32)
-    own_grad = widen_grad(grad_mant, grad_exp, order).reshape(4, 2, BLOCK, -1)
-
     other = send(act[1], core=1)
-    grad_c = send(own_grad, core=1)
-    grad_z = send(own_grad, z=1)
-    grad_zc = send(grad_z, core=1)
-    grads = jnp.stack(
-        [
-            jnp.stack([own_grad, grad_c], axis=2),
-            jnp.stack([grad_z, grad_zc], axis=2),
-        ],
-        axis=1,
-    ).reshape(4, 8 * BLOCK, -1)
-
-    width = grads.shape[-1]
+    (grad_mant,) = tied((grad_mant,), act)
+    own = widen_grad(grad_mant, grad_exp, order).reshape(4, 2, BLOCK, -1)
+    width = own.shape[-1]
     half = width // 2
-    rows = []
-    for k in range(PARTS):
-        here, there = (
-            jnp.concatenate([act[0, flip, k], other[flip, k]], axis=0) for flip in range(2)
-        )
-        piece = jnp.concatenate(
-            [here, send(here, z=2), send(there, z=1), send(there, z=3)], axis=0
-        )
-        mid = piece.shape[0] // 2
-        behind = send(piece, y=1)
-        ahead = send(piece, y=3)
-        far = jnp.concatenate([send(behind[:mid], y=1), send(ahead[mid:], y=3)], axis=0)
-        total = contract(piece, grads[0]) + contract(ahead, grads[1])
-        total = total + contract(behind, grads[3]) + contract(far, grads[2])
-        total = total.reshape(4, BLOCK, width)
-        first = send(total[2, :, :half], x=1)
-        second = send(total[2, :, half:], x=3)
-        to_next = jnp.concatenate([total[1, :, :half] + first, total[1, :, half:]], axis=1)
-        to_last = jnp.concatenate([total[3, :, :half], total[3, :, half:] + second], axis=1)
-        rows.append(total[0] + send(to_next, x=1) + send(to_last, x=3))
+    tokens = 4 * BLOCK
+
+    def joined(first, second):
+        return jnp.stack([first, second], axis=2).reshape(4, tokens, width)
+
+    def first_x(total):
+        return send(total[..., 2, :, :half], x=1), send(total[..., 2, :, half:], x=3)
+
+    def second_x(total, first, second):
+        up, down = total[..., 1, :, :], total[..., 3, :, :]
+        up = jnp.concatenate([up[..., :half] + first, up[..., half:]], axis=-1)
+        down = jnp.concatenate([down[..., :half], down[..., half:] + second], axis=-1)
+        return send(up, x=1), send(down, x=3)
+
+    pair = jnp.concatenate([act[0, :, 0], other[:, 0]], axis=1)
+    (for_core,) = tied((own,), other)
+    piece0 = jnp.concatenate([pair, send(pair, z=2)], axis=1)
+    own_c = send(for_core, core=1)
+    piece0, mine, other = tied((piece0, act[0], other), own_c)
+    behind0, ahead0 = send(piece0, y=1), send(piece0, y=3)
+    pairs = jnp.concatenate([mine[:, 1:], other[:, 1:]], axis=2)
+    here, there = pairs[0], pairs[1]
+    pieces = jnp.concatenate(
+        [here, send(here, z=2), send(there, z=1), send(there, z=3)], axis=1
+    )
+    behind0, ahead0, pieces, for_z = tied((behind0, ahead0, pieces, own))
+    far0 = [send(behind0[0], y=1), send(ahead0[1], y=3)]
+    near = [send(for_z[:1], z=1)]
+    piece1, for_z, *far0 = tied((pieces[0], for_z, *far0, *near))[:4]
+    near.append(send(for_z[1:], z=1))
+    behind1, ahead1 = send(piece1, y=1), send(piece1, y=3)
+
+    grads = joined(own, own_c)
+
+    def with_own(steps):
+        total = contract(steps[0], grads[0])
+        for step in range(1, 4):
+            if steps[step] is not None:
+                total = total + contract(steps[step], grads[step])
+        return total
+
+    total0 = jnp.stack(
+        [with_own([piece0[i], ahead0[i], far0[i], behind0[i]]) for i in range(2)]
+    ).reshape(2, 4, BLOCK, width)
+    x0 = first_x(total0)
+    w0 = second_x(total0, *x0)
+    behind1, ahead1 = tied((behind1, ahead1), *x0)
+    far1 = [send(behind1[:tokens], y=1), send(ahead1[tokens:], y=3)]
+    piece2, *near, far10, far11, w00, w01 = tied((pieces[1], *near, *far1, *w0))
+    far1, w0 = (far10, far11), (w00, w01)
+    near = jnp.concatenate(near, axis=0)
+    behind2, ahead2 = send(piece2, y=1), send(piece2, y=3)
+    near_c = send(near, core=1)
+    near_grads = joined(near, near_c)
+
+    def with_near(total, steps):
+        for step in range(4):
+            if steps[step] is not None:
+                total = total + contract(steps[step], near_grads[step])
+        return total
+
+    def begun(piece, ahead, behind):
+        total = with_own([piece[:tokens], ahead[:tokens], None, behind[:tokens]])
+        return with_near(total, [piece[tokens:], ahead[tokens:], None, behind[tokens:]])
+
+    def ended(total, far):
+        total = total + contract(far[0], grads[2]) + contract(far[1], near_grads[2])
+        return total.reshape(4, BLOCK, width)
+
+    total1 = begun(piece1, ahead1, behind1)
+    total1 = ended(total1, far1)
+    x1 = first_x(total1)
+    sums0 = total0[:, 0] + w0[0] + w0[1]
+    across0 = send(sums0[1], z=1)
+    behind2, ahead2, across0, *x1 = tied((behind2, ahead2, across0, *x1))
+    far2 = [send(behind2[:tokens], y=1), send(ahead2[tokens:], y=3)]
+    w1 = second_x(total1, *x1)
+    total2 = begun(piece2, ahead2, behind2)
+    total2, *far2 = tied((total2, *far2))
+    total2 = ended(total2, far2)
+    x2 = first_x(total2)
+    w10, w11, *x2 = tied((*w1, *x2))
+    w1 = w10, w11
+    w2 = second_x(total2, *x2)
+    rows = [sums0[0] + across0] + [
+        total[0] + w[0] + w[1] for total, w in ((total1, w1), (total2, w2))
+    ]
     return jnp.concatenate(rows, axis=0)
 
 

time: 243 us -> 183 us (0.75)
  waiting for transfers between devices: 164 us -> 101 us
  matrix products: 15.7 us -> 18.3 us
    ppermute x37 -> x34, waiting for transfers between devices: 164 us -> 101 us  [send(): return lax.ppermute(value, AXES, pairs)]
    dot_general x12 -> x24, matrix products: 15.7 us -> 18.3 us  [contract(): lax.dot_general(left, right, (((0,), (0,)), ((), ())), preferred_element_...]
    ppermute x37 -> x34, starting transfers between devices: 50.1 us -> 48 us  [send(): return lax.ppermute(value, AXES, pairs)]
  transfers between devices with their start and end apart: 37 -> 34, of which waited for: 21 -> 18; matrix products, arithmetic and copies ran while one was open for 8% -> 9% of each run, Pallas kernels for 0% -> 1%
where the time goes in v3:
time: 183 us; the launch traced here: 182 us
  waiting for transfers between devices  101 us (55%)
  starting transfers between devices  48 us (26%)
  matrix products  18.3 us (10%)
  local copies, waits for them, and re-layouts  6.61 us (4%)
  other arithmetic  5.02 us (3%)
  Pallas kernels  2.56 us (1%)
    ppermute x34, waiting for transfers between devices, send(): return lax.ppermute(value, AXES, pairs)  101 us
    ppermute x34, starting transfers between devices, send(): return lax.ppermute(value, AXES, pairs)  48 us
    dot_general x24, matrix products, contract(): lax.dot_general(left, right, (((0,), (0,)), ((), ())), preferred_element_...  18.3 us
    unnamed x7, local copies, waits for them, and re-layouts  4.12 us
  transfers between devices with their start and end apart: 34, of which 18 were waited for; matrix products, arithmetic and copies ran while one was open for 9% of the time, Pallas kernels for 1%

profile of v3, /device:TPU:6, one launch (start us, length us, event | category | flops | bytes accessed | tf_op | source)
XLA Modules:
  0.0 182.5 jit_solution(5860328300474002169)
XLA Ops:
  1.0 1.9 %copy-done.1 = s32[128,6144]{1,0:T(8,128)S(1)} copy-done((s32[128,6144]{1,0:T(8,128)S(1)}, s32[128,6144]{1,0:T(8,128)}, u32[]{:S(2)}) %copy-start.1) | copy-done | bytes 3145752
  5.5 2.2 %copy-done = s32[1024,1024]{1,0:T(8,128)S(1)} copy-done((s32[1024,1024]{1,0:T(8,128)S(1)}, s32[1024,1024]{1,0:T(8,128)}, u32[]{:S(2)}) %copy-start) | copy-done | bytes 4194328
  9.5 4.0 %collective-permute-start.1 = (bf16[2,256,512]{2,1,0:T(8,128)(2,1)S(1)}, bf16[2,256,512]{2,1,0:T(8,128)(2,1)S(1)}, u32[]{:S(2)}, u32[]{:S(2)}) collective-permute-start(bf16[2,256,512]{2,1,0:T(8,128)(2,1)S(1)} %pad_maximum_fusion.9), channel_id=1, source_target_pairs={{0,4},{1,5},{2,6},{3,7},{4,0},{5,1},{6,2},{7,3},{8,12},{9,13},{10,... | collective-permute-start | bytes 1572872 | tf_op jit(solution)/shard_map/ppermute | solution.py:27
  13.4 12.1 %collective-permute-done.1 = bf16[2,256,512]{2,1,0:T(8,128)(2,1)S(1)} collective-permute-done((bf16[2,256,512]{2,1,0:T(8,128)(2,1)S(1)}, bf16[2,256,512]{2,1,0:T(8,128)(2,1)S(1)}, u32[]{:S(2)}, u32[]{:S(2)}) %collective-permute-start.1) | collective-permute-done | bytes 524320 | tf_op jit(solution)/shard_map/ppermute | solution.py:27
  27.1 2.5 %collective-permute-start.7 = (bf16[2,256,512]{2,1,0:T(8,128)(2,1)S(1)}, bf16[2,256,512]{2,1,0:T(8,128)(2,1)S(1)}, u32[]{:S(2)}, u32[]{:S(2)}) collective-permute-start(bf16[2,256,512]{2,1,0:T(8,128)(2,1)S(1)} %get-tuple-element.106), channel_id=1, source_target_pairs={{0,20},{1,21},{2,22},{3,23},{4,16},{5,17},{6,18},{7,19},{8,28},{9,... | collective-permute-start | bytes 1572872 | tf_op jit(solution)/shard_map/ppermute | solution.py:27
  31.2 1.7 collective-permute-start.4
  35.8 17.1 %collective-permute-done.5 = bf16[2,256,512]{2,1,0:T(8,128)(2,1)S(1)} collective-permute-done((bf16[2,256,512]{2,1,0:T(8,128)(2,1)S(1)}, bf16[2,256,512]{2,1,0:T(8,128)(2,1)S(1)}, u32[]{:S(2)}, u32[]{:S(2)}) %collective-permute-start.5) | collective-permute-done | bytes 524320 | tf_op jit(solution)/shard_map/ppermute | solution.py:27
  56.6 1.6 collective-permute-start.8
  58.2 1.7 collective-permute-start.9
  60.8 6.3 %collective-permute-done.10 = bf16[1,2,128,1024]{3,2,1,0:T(8,128)(2,1)S(1)} collective-permute-done((bf16[1,2,128,1024]{3,2,1,0:T(8,128)(2,1)S(1)}, bf16[1,2,128,1024]{3,2,1,0:T(8,128)(2,1)S(1)}, u32[]{:S(2)}, u32[]{:S(2)}) %collective-permute-start.10) | collective-permute-done | bytes 524320 | tf_op jit(solution)/shard_map/ppermute | solution.py:27
  67.1 2.1 %collective-permute-done.8 = bf16[512,512]{1,0:T(8,128)(2,1)S(1)} collective-permute-done((bf16[512,512]{1,0:T(8,128)(2,1)S(1)}, bf16[512,512]{1,0:T(8,128)(2,1)S(1)}, u32[]{:S(2)}, u32[]{:S(2)}) %collective-permute-start.8) | collective-permute-done | bytes 524320 | tf_op jit(solution)/shard_map/ppermute | solution.py:27
  75.5 2.2 %collective-permute-start.13 = (bf16[1024,512]{1,0:T(8,128)(2,1)S(1)}, bf16[1024,512]{1,0:T(8,128)(2,1)S(1)}, u32[]{:S(2)}, u32[]{:S(2)}) collective-permute-start(bf16[1024,512]{1,0:T(8,128)(2,1)S(1)} %get-tuple-element.51), channel_id=1, source_target_pairs={{0,3},{1,0},{2,1},{3,2},{4,7},{5,4},{6,5},{7,6},{8,11},{9,8},{10,9... | collective-permute-start | bytes 3145736 | tf_op jit(solution)/shard_map/ppermute | solution.py:27
  79.4 3.4 %collective-permute-done.14 = f32[2,128,512]{2,1,0:T(8,128)S(1)} collective-permute-done((f32[2,128,512]{2,1,0:T(8,128)S(1)}, f32[2,128,512]{2,1,0:T(8,128)S(1)}, u32[]{:S(2)}, u32[]{:S(2)}) %collective-permute-start.14) | collective-permute-done | bytes 524320 | tf_op jit(solution)/shard_map/ppermute | solution.py:27
  82.7 1.7 collective-permute-done.15
  86.6 1.8 collective-permute-start.18
  88.3 9.3 %collective-permute-done.12 = bf16[1024,512]{1,0:T(8,128)(2,1)S(1)} collective-permute-done((bf16[1024,512]{1,0:T(8,128)(2,1)S(1)}, bf16[1024,512]{1,0:T(8,128)(2,1)S(1)}, u32[]{:S(2)}, u32[]{:S(2)}) %collective-permute-start.12) | collective-permute-done | bytes 1048608 | tf_op jit(solution)/shard_map/ppermute | solution.py:27
  98.5 2.6 %collective-permute-start.17 = (bf16[512,512]{1,0:T(8,128)(2,1)S(1)}, bf16[512,512]{1,0:T(8,128)(2,1)S(1)}, u32[]{:S(2)}, u32[]{:S(2)}) collective-permute-start(bf16[512,512]{1,0:T(8,128)(2,1)S(1)} %slice.263), channel_id=1, source_target_pairs={{0,3},{1,0},{2,1},{3,2},{4,7},{5,4},{6,5},{7,6},{8,11},{9,8},{10,9... | collective-permute-start | bytes 1572872 | tf_op jit(solution)/shard_map/ppermute | solution.py:27
  101.1 5.5 %collective-permute-done.19 = f32[2,128,1024]{2,1,0:T(8,128)S(1)} collective-permute-done((f32[2,128,1024]{2,1,0:T(8,128)S(1)}, f32[2,128,1024]{2,1,0:T(8,128)S(1)}, u32[]{:S(2)}, u32[]{:S(2)}) %collective-permute-start.19) | collective-permute-done | bytes 1048608 | tf_op jit(solution)/shard_map/ppermute | solution.py:27
  108.1 1.7 collective-permute-done.11
  112.4 3.2 %collective-permute-start.21 = (bf16[1024,512]{1,0:T(8,128)(2,1)S(1)}, bf16[1024,512]{1,0:T(8,128)(2,1)S(1)}, u32[]{:S(2)}, u32[]{:S(2)}) collective-permute-start(bf16[1024,512]{1,0:T(8,128)(2,1)S(1)} %get-tuple-element.56), channel_id=1, source_target_pairs={{0,3},{1,0},{2,1},{3,2},{4,7},{5,4},{6,5},{7,6},{8,11},{9,8},{10,9... | collective-permute-start | bytes 3145736 | tf_op jit(solution)/shard_map/ppermute | solution.py:27
  122.6 1.8 collective-permute-start.24
  125.4 4.4 %collective-permute-done.22 = f32[128,1024]{1,0:T(8,128)S(1)} collective-permute-done((f32[128,1024]{1,0:T(8,128)S(1)}, f32[128,1024]{1,0:T(8,128)S(1)}, u32[]{:S(2)}, u32[]{:S(2)}) %collective-permute-start.22) | collective-permute-done | bytes 524320 | tf_op jit(solution)/shard_map/ppermute | solution.py:27
  129.8 9.4 %collective-permute-done.20 = bf16[1024,512]{1,0:T(8,128)(2,1)S(1)} collective-permute-done((bf16[1024,512]{1,0:T(8,128)(2,1)S(1)}, bf16[1024,512]{1,0:T(8,128)(2,1)S(1)}, u32[]{:S(2)}, u32[]{:S(2)}) %collective-permute-start.20) | collective-permute-done | bytes 1048608 | tf_op jit(solution)/shard_map/ppermute | solution.py:27
  141.6 3.2 %collective-permute-start.29 = (bf16[512,512]{1,0:T(8,128)(2,1)S(1)}, bf16[512,512]{1,0:T(8,128)(2,1)S(1)}, u32[]{:S(2)}, u32[]{:S(2)}) collective-permute-start(bf16[512,512]{1,0:T(8,128)(2,1)S(1)} %slice.291), channel_id=1, source_target_pairs={{0,3},{1,0},{2,1},{3,2},{4,7},{5,4},{6,5},{7,6},{8,11},{9,8},{10,9... | collective-permute-start | bytes 1572872 | tf_op jit(solution)/shard_map/ppermute | solution.py:27
  145.9 2.5 %collective-permute-start.26 = (f32[128,1024]{1,0:T(8,128)S(1)}, f32[128,1024]{1,0:T(8,128)S(1)}, u32[]{:S(2)}, u32[]{:S(2)}) collective-permute-start(f32[128,1024]{1,0:T(8,128)S(1)} %pad_maximum_fusion.10), channel_id=1, source_target_pairs={{0,32},{1,33},{2,34},{3,35},{4,36},{5,37},{6,38},{7,39},{8,40},{9,... | collective-permute-start | bytes 1572872 | tf_op jit(solution)/shard_map/ppermute | solution.py:27
  149.5 6.8 %collective-permute-done.28 = bf16[512,512]{1,0:T(8,128)(2,1)S(1)} collective-permute-done((bf16[512,512]{1,0:T(8,128)(2,1)S(1)}, bf16[512,512]{1,0:T(8,128)(2,1)S(1)}, u32[]{:S(2)}, u32[]{:S(2)}) %collective-permute-start.28) | collective-permute-done | bytes 524320 | tf_op jit(solution)/shard_map/ppermute | solution.py:27
  157.8 1.8 collective-permute-start.30
  159.9 5.0 %collective-permute-done.30 = f32[128,512]{1,0:T(8,128)S(1)} collective-permute-done((f32[128,512]{1,0:T(8,128)S(1)}, f32[128,512]{1,0:T(8,128)S(1)}, u32[]{:S(2)}, u32[]{:S(2)}) %collective-permute-start.30) | collective-permute-done | bytes 262176 | tf_op jit(solution)/shard_map/ppermute | solution.py:27
  164.9 2.6 %collective-permute-done.31 = f32[128,512]{1,0:T(8,128)S(1)} collective-permute-done((f32[128,512]{1,0:T(8,128)S(1)}, f32[128,512]{1,0:T(8,128)S(1)}, u32[]{:S(2)}, u32[]{:S(2)}) %collective-permute-start.31) | collective-permute-done | bytes 262176 | tf_op jit(solution)/shard_map/ppermute | solution.py:27
  168.3 1.7 collective-permute-start.33
  170.2 9.1 %collective-permute-done.32 = f32[128,1024]{1,0:T(8,128)S(1)} collective-permute-done((f32[128,1024]{1,0:T(8,128)S(1)}, f32[128,1024]{1,0:T(8,128)S(1)}, u32[]{:S(2)}, u32[]{:S(2)}) %collective-permute-start.32) | collective-permute-done | bytes 524320 | tf_op jit(solution)/shard_map/ppermute | solution.py:27
  179.3 1.8 collective-permute-done.33
  (120 shorter events, 47.4 us)
Async XLA Ops:
  8.8 16.8 %collective-permute-start.2 = (bf16[4,2,128,1024]{3,2,1,0:T(8,128)(2,1)S(1)}, bf16[4,2,128,1024]{3,2,1,0:T(8,128)(2,1)S(1)}, u32[]{:S(2)}, u32[]{:S(2)}) collective-permute-start(bf16[4,2,128,1024]{3,2,1,0:T(8,128)(2,1)S(1)} %bitcast.132), channel_id=1, source_target_pairs={{0,8},{1,9},{2,10},{3,11},{4,12},{5,13},{6,14},{7,15},{8,0},{9,1},... | collective-permute-start | bytes 6291464 | tf_op jit(solution)/shard_map/ppermute | solution.py:27
  9.5 16.1 %collective-permute-start.1 = (bf16[2,256,512]{2,1,0:T(8,128)(2,1)S(1)}, bf16[2,256,512]{2,1,0:T(8,128)(2,1)S(1)}, u32[]{:S(2)}, u32[]{:S(2)}) collective-permute-start(bf16[2,256,512]{2,1,0:T(8,128)(2,1)S(1)} %pad_maximum_fusion.9), channel_id=1, source_target_pairs={{0,4},{1,5},{2,6},{3,7},{4,0},{5,1},{6,2},{7,3},{8,12},{9,13},{10,... | collective-permute-start | bytes 1572872 | tf_op jit(solution)/shard_map/ppermute | solution.py:27
  25.8 27.2 %collective-permute-start.6 = (bf16[2,256,512]{2,1,0:T(8,128)(2,1)S(1)}, bf16[2,256,512]{2,1,0:T(8,128)(2,1)S(1)}, u32[]{:S(2)}, u32[]{:S(2)}) collective-permute-start(bf16[2,256,512]{2,1,0:T(8,128)(2,1)S(1)} %get-tuple-element.106), channel_id=1, source_target_pairs={{0,16},{1,17},{2,18},{3,19},{4,20},{5,21},{6,22},{7,23},{8,24},{9,... | collective-permute-start | bytes 1572872 | tf_op jit(solution)/shard_map/ppermute | solution.py:27
  27.1 25.8 %collective-permute-start.7 = (bf16[2,256,512]{2,1,0:T(8,128)(2,1)S(1)}, bf16[2,256,512]{2,1,0:T(8,128)(2,1)S(1)}, u32[]{:S(2)}, u32[]{:S(2)}) collective-permute-start(bf16[2,256,512]{2,1,0:T(8,128)(2,1)S(1)} %get-tuple-element.106), channel_id=1, source_target_pairs={{0,20},{1,21},{2,22},{3,23},{4,16},{5,17},{6,18},{7,19},{8,28},{9,... | collective-permute-start | bytes 1572872 | tf_op jit(solution)/shard_map/ppermute | solution.py:27
  29.7 24.9 %collective-permute-start.3 = (bf16[2,512,512]{2,1,0:T(8,128)(2,1)S(1)}, bf16[2,512,512]{2,1,0:T(8,128)(2,1)S(1)}, u32[]{:S(2)}, u32[]{:S(2)}) collective-permute-start(bf16[2,512,512]{2,1,0:T(8,128)(2,1)S(1)} %pad_maximum_fusion.5), channel_id=1, source_target_pairs={{0,1},{1,2},{2,3},{3,0},{4,5},{5,6},{6,7},{7,4},{8,9},{9,10},{10,1... | collective-permute-start | bytes 3145736 | tf_op jit(solution)/shard_map/ppermute | solution.py:27
  31.2 23.4 %collective-permute-start.4 = (bf16[2,512,512]{2,1,0:T(8,128)(2,1)S(1)}, bf16[2,512,512]{2,1,0:T(8,128)(2,1)S(1)}, u32[]{:S(2)}, u32[]{:S(2)}) collective-permute-start(bf16[2,512,512]{2,1,0:T(8,128)(2,1)S(1)} %pad_maximum_fusion.5), channel_id=1, source_target_pairs={{0,3},{1,0},{2,1},{3,2},{4,7},{5,4},{6,5},{7,6},{8,11},{9,8},{10,9... | collective-permute-start | bytes 3145736 | tf_op jit(solution)/shard_map/ppermute | solution.py:27
  32.9 20.0 %collective-permute-start.5 = (bf16[2,256,512]{2,1,0:T(8,128)(2,1)S(1)}, bf16[2,256,512]{2,1,0:T(8,128)(2,1)S(1)}, u32[]{:S(2)}, u32[]{:S(2)}) collective-permute-start(bf16[2,256,512]{2,1,0:T(8,128)(2,1)S(1)} %get-tuple-element.105), channel_id=1, source_target_pairs={{0,4},{1,5},{2,6},{3,7},{4,0},{5,1},{6,2},{7,3},{8,12},{9,13},{10,... | collective-permute-start | bytes 1572872 | tf_op jit(solution)/shard_map/ppermute | solution.py:27
  55.4 11.6 %collective-permute-start.10 = (bf16[1,2,128,1024]{3,2,1,0:T(8,128)(2,1)S(1)}, bf16[1,2,128,1024]{3,2,1,0:T(8,128)(2,1)S(1)}, u32[]{:S(2)}, u32[]{:S(2)}) collective-permute-start(bf16[1,2,128,1024]{3,2,1,0:T(8,128)(2,1)S(1)} %slice.252), channel_id=1, source_target_pairs={{0,16},{1,17},{2,18},{3,19},{4,20},{5,21},{6,22},{7,23},{8,24},{9,... | collective-permute-start | bytes 1572872 | tf_op jit(solution)/shard_map/ppermute | solution.py:27
  56.6 12.6 %collective-permute-start.8 = (bf16[512,512]{1,0:T(8,128)(2,1)S(1)}, bf16[512,512]{1,0:T(8,128)(2,1)S(1)}, u32[]{:S(2)}, u32[]{:S(2)}) collective-permute-start(bf16[512,512]{1,0:T(8,128)(2,1)S(1)} %slice_bitcast_fusion.7), channel_id=1, source_target_pairs={{0,1},{1,2},{2,3},{3,0},{4,5},{5,6},{6,7},{7,4},{8,9},{9,10},{10,1... | collective-permute-start | bytes 1572872 | tf_op jit(solution)/shard_map/ppermute | solution.py:27
  58.2 10.9 %collective-permute-start.9 = (bf16[512,512]{1,0:T(8,128)(2,1)S(1)}, bf16[512,512]{1,0:T(8,128)(2,1)S(1)}, u32[]{:S(2)}, u32[]{:S(2)}) collective-permute-start(bf16[512,512]{1,0:T(8,128)(2,1)S(1)} %slice_bitcast_fusion.6), channel_id=1, source_target_pairs={{0,3},{1,0},{2,1},{3,2},{4,7},{5,4},{6,5},{7,6},{8,11},{9,8},{10,9... | collective-permute-start | bytes 1572872 | tf_op jit(solution)/shard_map/ppermute | solution.py:27
  72.3 10.4 %collective-permute-start.14 = (f32[2,128,512]{2,1,0:T(8,128)S(1)}, f32[2,128,512]{2,1,0:T(8,128)S(1)}, u32[]{:S(2)}, u32[]{:S(2)}) collective-permute-start(f32[2,128,512]{2,1,0:T(8,128)S(1)} %get-tuple-element.80), channel_id=1, source_target_pairs={{0,32},{1,33},{2,34},{3,35},{4,36},{5,37},{6,38},{7,39},{8,40},{9,... | collective-permute-start | bytes 1572872 | tf_op jit(solution)/shard_map/ppermute | solution.py:27
  72.9 11.6 %collective-permute-start.15 = (f32[2,128,512]{2,1,0:T(8,128)S(1)}, f32[2,128,512]{2,1,0:T(8,128)S(1)}, u32[]{:S(2)}, u32[]{:S(2)}) collective-permute-start(f32[2,128,512]{2,1,0:T(8,128)S(1)} %get-tuple-element.79), channel_id=1, source_target_pairs={{0,96},{1,97},{2,98},{3,99},{4,100},{5,101},{6,102},{7,103},{8,104... | collective-permute-start | bytes 1572872 | tf_op jit(solution)/shard_map/ppermute | solution.py:27
  74.4 23.2 %collective-permute-start.12 = (bf16[1024,512]{1,0:T(8,128)(2,1)S(1)}, bf16[1024,512]{1,0:T(8,128)(2,1)S(1)}, u32[]{:S(2)}, u32[]{:S(2)}) collective-permute-start(bf16[1024,512]{1,0:T(8,128)(2,1)S(1)} %get-tuple-element.51), channel_id=1, source_target_pairs={{0,1},{1,2},{2,3},{3,0},{4,5},{5,6},{6,7},{7,4},{8,9},{9,10},{10,1... | collective-permute-start | bytes 3145736 | tf_op jit(solution)/shard_map/ppermute | solution.py:27
  75.5 22.2 %collective-permute-start.13 = (bf16[1024,512]{1,0:T(8,128)(2,1)S(1)}, bf16[1024,512]{1,0:T(8,128)(2,1)S(1)}, u32[]{:S(2)}, u32[]{:S(2)}) collective-permute-start(bf16[1024,512]{1,0:T(8,128)(2,1)S(1)} %get-tuple-element.51), channel_id=1, source_target_pairs={{0,3},{1,0},{2,1},{3,2},{4,7},{5,4},{6,5},{7,6},{8,11},{9,8},{10,9... | collective-permute-start | bytes 3145736 | tf_op jit(solution)/shard_map/ppermute | solution.py:27
  77.9 32.0 %collective-permute-start.11 = (bf16[3,2,128,1024]{3,2,1,0:T(8,128)(2,1)S(1)}, bf16[3,2,128,1024]{3,2,1,0:T(8,128)(2,1)S(1)}, u32[]{:S(2)}, u32[]{:S(2)}) collective-permute-start(bf16[3,2,128,1024]{3,2,1,0:T(8,128)(2,1)S(1)} %slice.259), channel_id=1, source_target_pairs={{0,16},{1,17},{2,18},{3,19},{4,20},{5,21},{6,22},{7,23},{8,24},{9,... | collective-permute-start | bytes 4718600 | tf_op jit(solution)/shard_map/ppermute | solution.py:27
  84.9 21.7 %collective-permute-start.19 = (f32[2,128,1024]{2,1,0:T(8,128)S(1)}, f32[2,128,1024]{2,1,0:T(8,128)S(1)}, u32[]{:S(2)}, u32[]{:S(2)}) collective-permute-start(f32[2,128,1024]{2,1,0:T(8,128)S(1)} %pad_maximum_fusion.7), channel_id=1, source_target_pairs={{0,96},{1,97},{2,98},{3,99},{4,100},{5,101},{6,102},{7,103},{8,104... | collective-permute-start | bytes 3145736 | tf_op jit(solution)/shard_map/ppermute | solution.py:27
  86.6 20.1 %collective-permute-start.18 = (f32[2,128,1024]{2,1,0:T(8,128)S(1)}, f32[2,128,1024]{2,1,0:T(8,128)S(1)}, u32[]{:S(2)}, u32[]{:S(2)}) collective-permute-start(f32[2,128,1024]{2,1,0:T(8,128)S(1)} %pad_maximum_fusion.6), channel_id=1, source_target_pairs={{0,32},{1,33},{2,34},{3,35},{4,36},{5,37},{6,38},{7,39},{8,40},{9,... | collective-permute-start | bytes 3145736 | tf_op jit(solution)/shard_map/ppermute | solution.py:27
  97.7 10.5 %collective-permute-start.16 = (bf16[512,512]{1,0:T(8,128)(2,1)S(1)}, bf16[512,512]{1,0:T(8,128)(2,1)S(1)}, u32[]{:S(2)}, u32[]{:S(2)}) collective-permute-start(bf16[512,512]{1,0:T(8,128)(2,1)S(1)} %slice.262), channel_id=1, source_target_pairs={{0,1},{1,2},{2,3},{3,0},{4,5},{5,6},{6,7},{7,4},{8,9},{9,10},{10,1... | collective-permute-start | bytes 1572872 | tf_op jit(solution)/shard_map/ppermute | solution.py:27
  98.5 9.6 %collective-permute-start.17 = (bf16[512,512]{1,0:T(8,128)(2,1)S(1)}, bf16[512,512]{1,0:T(8,128)(2,1)S(1)}, u32[]{:S(2)}, u32[]{:S(2)}) collective-permute-start(bf16[512,512]{1,0:T(8,128)(2,1)S(1)} %slice.263), channel_id=1, source_target_pairs={{0,3},{1,0},{2,1},{3,2},{4,7},{5,4},{6,5},{7,6},{8,11},{9,8},{10,9... | collective-permute-start | bytes 1572872 | tf_op jit(solution)/shard_map/ppermute | solution.py:27
  110.1 8.5 %collective-permute-start.23 = (bf16[4,2,128,1024]{3,2,1,0:T(8,128)(2,1)S(1)}, bf16[4,2,128,1024]{3,2,1,0:T(8,128)(2,1)S(1)}, u32[]{:S(2)}, u32[]{:S(2)}) collective-permute-start(bf16[4,2,128,1024]{3,2,1,0:T(8,128)(2,1)S(1)} %constant_dynamic-update-slice_fusion), channel_id=1, source_target_pairs={{0,8},{1,9},{2,10},{3,11},{4,12},{5,13},{6,14},{7,15},{8,0},{9,1},... | collective-permute-start | bytes 6291464 | tf_op jit(solution)/shard_map/ppermute | solution.py:27
  112.4 26.8 %collective-permute-start.20 = (bf16[1024,512]{1,0:T(8,128)(2,1)S(1)}, bf16[1024,512]{1,0:T(8,128)(2,1)S(1)}, u32[]{:S(2)}, u32[]{:S(2)}) collective-permute-start(bf16[1024,512]{1,0:T(8,128)(2,1)S(1)} %get-tuple-element.56), channel_id=1, source_target_pairs={{0,1},{1,2},{2,3},{3,0},{4,5},{5,6},{6,7},{7,4},{8,9},{9,10},{10,1... | collective-permute-start | bytes 3145736 | tf_op jit(solution)/shard_map/ppermute | solution.py:27
  112.4 26.8 %collective-permute-start.21 = (bf16[1024,512]{1,0:T(8,128)(2,1)S(1)}, bf16[1024,512]{1,0:T(8,128)(2,1)S(1)}, u32[]{:S(2)}, u32[]{:S(2)}) collective-permute-start(bf16[1024,512]{1,0:T(8,128)(2,1)S(1)} %get-tuple-element.56), channel_id=1, source_target_pairs={{0,3},{1,0},{2,1},{3,2},{4,7},{5,4},{6,5},{7,6},{8,11},{9,8},{10,9... | collective-permute-start | bytes 3145736 | tf_op jit(solution)/shard_map/ppermute | solution.py:27
  116.0 13.8 %collective-permute-start.22 = (f32[128,1024]{1,0:T(8,128)S(1)}, f32[128,1024]{1,0:T(8,128)S(1)}, u32[]{:S(2)}, u32[]{:S(2)}) collective-permute-start(f32[128,1024]{1,0:T(8,128)S(1)} %slice_bitcast_fusion.4), channel_id=1, source_target_pairs={{0,16},{1,17},{2,18},{3,19},{4,20},{5,21},{6,22},{7,23},{8,24},{9,... | collective-permute-start | bytes 1572872 | tf_op jit(solution)/shard_map/ppermute | solution.py:27
  122.6 16.6 %collective-permute-start.24 = (f32[128,512]{1,0:T(8,128)S(1)}, f32[128,512]{1,0:T(8,128)S(1)}, u32[]{:S(2)}, u32[]{:S(2)}) collective-permute-start(f32[128,512]{1,0:T(8,128)S(1)} %get-tuple-element.96), channel_id=1, source_target_pairs={{0,32},{1,33},{2,34},{3,35},{4,36},{5,37},{6,38},{7,39},{8,40},{9,... | collective-permute-start | bytes 786440 | tf_op jit(solution)/shard_map/ppermute | solution.py:27
  124.4 14.8 %collective-permute-start.25 = (f32[128,512]{1,0:T(8,128)S(1)}, f32[128,512]{1,0:T(8,128)S(1)}, u32[]{:S(2)}, u32[]{:S(2)}) collective-permute-start(f32[128,512]{1,0:T(8,128)S(1)} %get-tuple-element.95), channel_id=1, source_target_pairs={{0,96},{1,97},{2,98},{3,99},{4,100},{5,101},{6,102},{7,103},{8,104... | collective-permute-start | bytes 786440 | tf_op jit(solution)/shard_map/ppermute | solution.py:27
  141.5 14.8 %collective-permute-start.28 = (bf16[512,512]{1,0:T(8,128)(2,1)S(1)}, bf16[512,512]{1,0:T(8,128)(2,1)S(1)}, u32[]{:S(2)}, u32[]{:S(2)}) collective-permute-start(bf16[512,512]{1,0:T(8,128)(2,1)S(1)} %slice.289), channel_id=1, source_target_pairs={{0,1},{1,2},{2,3},{3,0},{4,5},{5,6},{6,7},{7,4},{8,9},{9,10},{10,1... | collective-permute-start | bytes 1572872 | tf_op jit(solution)/shard_map/ppermute | solution.py:27
  141.6 14.7 %collective-permute-start.29 = (bf16[512,512]{1,0:T(8,128)(2,1)S(1)}, bf16[512,512]{1,0:T(8,128)(2,1)S(1)}, u32[]{:S(2)}, u32[]{:S(2)}) collective-permute-start(bf16[512,512]{1,0:T(8,128)(2,1)S(1)} %slice.291), channel_id=1, source_target_pairs={{0,3},{1,0},{2,1},{3,2},{4,7},{5,4},{6,5},{7,6},{8,11},{9,8},{10,9... | collective-permute-start | bytes 1572872 | tf_op jit(solution)/shard_map/ppermute | solution.py:27
  145.0 14.9 %collective-permute-start.27 = (f32[128,1024]{1,0:T(8,128)S(1)}, f32[128,1024]{1,0:T(8,128)S(1)}, u32[]{:S(2)}, u32[]{:S(2)}) collective-permute-start(f32[128,1024]{1,0:T(8,128)S(1)} %pad_maximum_fusion.11), channel_id=1, source_target_pairs={{0,96},{1,97},{2,98},{3,99},{4,100},{5,101},{6,102},{7,103},{8,104... | collective-permute-start | bytes 1572872 | tf_op jit(solution)/shard_map/ppermute | solution.py:27
  145.9 14.0 %collective-permute-start.26 = (f32[128,1024]{1,0:T(8,128)S(1)}, f32[128,1024]{1,0:T(8,128)S(1)}, u32[]{:S(2)}, u32[]{:S(2)}) collective-permute-start(f32[128,1024]{1,0:T(8,128)S(1)} %pad_maximum_fusion.10), channel_id=1, source_target_pairs={{0,32},{1,33},{2,34},{3,35},{4,36},{5,37},{6,38},{7,39},{8,40},{9,... | collective-permute-start | bytes 1572872 | tf_op jit(solution)/shard_map/ppermute | solution.py:27
  159.6 8.0 %collective-permute-start.31 = (f32[128,512]{1,0:T(8,128)S(1)}, f32[128,512]{1,0:T(8,128)S(1)}, u32[]{:S(2)}, u32[]{:S(2)}) collective-permute-start(f32[128,512]{1,0:T(8,128)S(1)} %get-tuple-element.89), channel_id=1, source_target_pairs={{0,96},{1,97},{2,98},{3,99},{4,100},{5,101},{6,102},{7,103},{8,104... | collective-permute-start | bytes 786440 | tf_op jit(solution)/shard_map/ppermute | solution.py:27
  167.8 11.5 %collective-permute-start.32 = (f32[128,1024]{1,0:T(8,128)S(1)}, f32[128,1024]{1,0:T(8,128)S(1)}, u32[]{:S(2)}, u32[]{:S(2)}) collective-permute-start(f32[128,1024]{1,0:T(8,128)S(1)} %pad_maximum_fusion.12), channel_id=1, source_target_pairs={{0,32},{1,33},{2,34},{3,35},{4,36},{5,37},{6,38},{7,39},{8,40},{9,... | collective-permute-start | bytes 1572872 | tf_op jit(solution)/shard_map/ppermute | solution.py:27
  168.3 12.8 %collective-permute-start.33 = (f32[128,1024]{1,0:T(8,128)S(1)}, f32[128,1024]{1,0:T(8,128)S(1)}, u32[]{:S(2)}, u32[]{:S(2)}) collective-permute-start(f32[128,1024]{1,0:T(8,128)S(1)} %pad_maximum_fusion.13), channel_id=1, source_target_pairs={{0,96},{1,97},{2,98},{3,99},{4,100},{5,101},{6,102},{7,103},{8,104... | collective-permute-start | bytes 1572872 | tf_op jit(solution)/shard_map/ppermute | solution.py:27
  (5 other events, 15.6 us)

commit v4 on v3

--- a/solution.py
+++ b/solution.py
@@ -7,6 +7,7 @@
 
 AXES = ("dp", "tensor")
 BLOCK = 128
+STEPS = (0, 1, 3, 2)
 PARTS = 3
 
 
@@ -96,7 +97,7 @@
 
     act = widen_act(act_mant, act_exp, jnp.stack([x, z_lo, core]).astype(jnp.int32))
     order = jnp.stack(
-        [(z_hi ^ flip) * 4 + (y + step) % 4 for step in range(4) for flip in range(2)]
+        [(z_hi ^ flip) * 4 + (y + step) % 4 for step in STEPS for flip in range(2)]
     ).astype(jnp.int32)
     other = send(act[1], core=1)
     (grad_mant,) = tied((grad_mant,), act)
@@ -106,7 +107,7 @@
     tokens = 4 * BLOCK
 
     def joined(first, second):
-        return jnp.stack([first, second], axis=2).reshape(4, tokens, width)
+        return jnp.stack([first, second], axis=2).reshape(-1, tokens, width)
 
     def first_x(total):
         return send(total[..., 2, :, :half], x=1), send(total[..., 2, :, half:], x=3)
@@ -119,77 +120,80 @@
 
     pair = jnp.concatenate([act[0, :, 0], other[:, 0]], axis=1)
     (for_core,) = tied((own,), other)
-    piece0 = jnp.concatenate([pair, send(pair, z=2)], axis=1)
     own_c = send(for_core, core=1)
-    piece0, mine, other = tied((piece0, act[0], other), own_c)
-    behind0, ahead0 = send(piece0, y=1), send(piece0, y=3)
-    pairs = jnp.concatenate([mine[:, 1:], other[:, 1:]], axis=2)
-    here, there = pairs[0], pairs[1]
-    pieces = jnp.concatenate(
-        [here, send(here, z=2), send(there, z=1), send(there, z=3)], axis=1
-    )
-    behind0, ahead0, pieces, for_z = tied((behind0, ahead0, pieces, own))
+    pair_z = send(pair, z=2)
+    behind0, ahead0 = [send(pair, y=1)], [send(pair, y=3)]
+    pair_z, mine, other, *_ = tied((pair_z, act[0], other), own_c, *behind0, *ahead0)
+    behind0, ahead0 = behind0 + [send(pair_z, y=1)], ahead0 + [send(pair_z, y=3)]
+
+    def along_z(k, mine, other):
+        here, there = (
+            jnp.concatenate([mine[flip, k], other[flip, k]], axis=0) for flip in range(2)
+        )
+        return jnp.concatenate(
+            [here, send(here, z=2), send(there, z=1), send(there, z=3)], axis=0
+        )
+
+    piece0, behind0, ahead0 = (
+        jnp.concatenate(parts, axis=1) for parts in ([pair, pair_z], behind0, ahead0)
+    )
+    pair = jnp.concatenate([mine[:, 1], other[:, 1]], axis=1)
+    piece1 = jnp.concatenate([pair, send(pair, z=2)], axis=1)
+    behind0, ahead0, piece1, mine, other = tied((behind0, ahead0, piece1, mine, other))
     far0 = [send(behind0[0], y=1), send(ahead0[1], y=3)]
+    piece2 = along_z(2, mine, other)
+    piece1, piece2, for_z, *far0 = tied((piece1, piece2, own, *far0))
+    behind1, ahead1 = send(piece1, y=1), send(piece1, y=3)
     near = [send(for_z[:1], z=1)]
-    piece1, for_z, *far0 = tied((pieces[0], for_z, *far0, *near))[:4]
-    near.append(send(for_z[1:], z=1))
-    behind1, ahead1 = send(piece1, y=1), send(piece1, y=3)
 
     grads = joined(own, own_c)
 
     def with_own(steps):
         total = contract(steps[0], grads[0])
-        for step in range(1, 4):
-            if steps[step] is not None:
-                total = total + contract(steps[step], grads[step])
+        for step in range(1, len(steps)):
+            total = total + contract(steps[step], grads[step])
         return total
 
-    total0 = jnp.stack(
-        [with_own([piece0[i], ahead0[i], far0[i], behind0[i]]) for i in range(2)]
-    ).reshape(2, 4, BLOCK, width)
+    def of_both(*steps):
+        return jnp.stack(
+            [with_own([part[i] for part in steps]) for i in range(2)]
+        ).reshape(2, 4, BLOCK, width)
+
+    total0 = of_both(piece0, ahead0, behind0, far0)
     x0 = first_x(total0)
     w0 = second_x(total0, *x0)
-    behind1, ahead1 = tied((behind1, ahead1), *x0)
-    far1 = [send(behind1[:tokens], y=1), send(ahead1[tokens:], y=3)]
-    piece2, *near, far10, far11, w00, w01 = tied((pieces[1], *near, *far1, *w0))
-    far1, w0 = (far10, far11), (w00, w01)
-    near = jnp.concatenate(near, axis=0)
+    behind1, ahead1, for_z, near0 = tied((behind1, ahead1, for_z, near[0]), *x0)
+    far1 = [send(behind1[0], y=1), send(ahead1[1], y=3)]
+    near1 = send(for_z[1:2], z=1)
+    piece2, for_z, near0, near1, far10, far11, w00, w01 = tied(
+        (piece2, for_z, near0, near1, *far1, *w0)
+    )
+    w0 = w00, w01
     behind2, ahead2 = send(piece2, y=1), send(piece2, y=3)
-    near_c = send(near, core=1)
+    near2 = send(for_z[2:], z=1)
+    total1 = of_both(piece1, ahead1, behind1, [far10, far11])
+    x1 = first_x(total1)
+    w1 = second_x(total1, *x1)
+    behind2, ahead2, near2 = tied((behind2, ahead2, near2), *x1)
+    far2 = [send(behind2[:tokens], y=1), send(ahead2[tokens:], y=3)]
+    near = jnp.concatenate([near0, near1, near2], axis=0)
+    sums0 = total0[:, 0] + w0[0] + w0[1]
+    for_across, near_c = tied((sums0[1], send(near, core=1)))
+    across0 = send(for_across, z=1)
     near_grads = joined(near, near_c)
-
-    def with_near(total, steps):
-        for step in range(4):
-            if steps[step] is not None:
-                total = total + contract(steps[step], near_grads[step])
-        return total
-
-    def begun(piece, ahead, behind):
-        total = with_own([piece[:tokens], ahead[:tokens], None, behind[:tokens]])
-        return with_near(total, [piece[tokens:], ahead[tokens:], None, behind[tokens:]])
-
-    def ended(total, far):
-        total = total + contract(far[0], grads[2]) + contract(far[1], near_grads[2])
-        return total.reshape(4, BLOCK, width)
-
-    total1 = begun(piece1, ahead1, behind1)
-    total1 = ended(total1, far1)
-    x1 = first_x(total1)
-    sums0 = total0[:, 0] + w0[0] + w0[1]
-    across0 = send(sums0[1], z=1)
-    behind2, ahead2, across0, *x1 = tied((behind2, ahead2, across0, *x1))
-    far2 = [send(behind2[:tokens], y=1), send(ahead2[tokens:], y=3)]
-    w1 = second_x(total1, *x1)
-    total2 = begun(piece2, ahead2, behind2)
-    total2, *far2 = tied((total2, *far2))
-    total2 = ended(total2, far2)
+    steps = piece2, ahead2, behind2
+    total2 = with_own([part[:tokens] for part in steps])
+    for step in range(3):
+        total2 = total2 + contract(steps[step][tokens:], near_grads[step])
+    total2, far20, far21, across0 = tied((total2, *far2, across0))
+    total2 = total2 + contract(far20, grads[3]) + contract(far21, near_grads[3])
+    total2 = total2.reshape(4, BLOCK, width)
     x2 = first_x(total2)
     w10, w11, *x2 = tied((*w1, *x2))
-    w1 = w10, w11
+    sums1 = total1[:, 0] + w10 + w11
+    across1 = send(sums1[1], z=1)
     w2 = second_x(total2, *x2)
-    rows = [sums0[0] + across0] + [
-        total[0] + w[0] + w[1] for total, w in ((total1, w1), (total2, w2))
-    ]
+    rows = [sums0[0] + across0, sums1[0] + across1, total2[0] + w2[0] + w2[1]]
     return jnp.concatenate(rows, axis=0)
 
 

time: 183 us -> 179 us (0.978)
  waiting for transfers between devices: 101 us -> 89 us
  starting transfers between devices: 48 us -> 56 us
    ppermute x34 -> x39, waiting for transfers between devices: 101 us -> 89 us  [send(): return lax.ppermute(value, AXES, pairs)]
    ppermute x34 -> x39, starting transfers between devices: 48 us -> 56 us  [send(): return lax.ppermute(value, AXES, pairs)]
    unnamed x7 -> x12, local copies, waits for them, and re-layouts: 4.12 us -> 4.22 us
  transfers between devices with their start and end apart: 34 -> 39, of which waited for: 18 -> 20; matrix products, arithmetic and copies ran while one was open for 9% -> 12% of each run, Pallas kernels for 1% -> 1%
where the time goes in v4:
time: 179 us; the launch traced here: 178 us
  waiting for transfers between devices  89 us (50%)
  starting transfers between devices  56 us (31%)
  matrix products  18.2 us (10%)
  local copies, waits for them, and re-layouts  6.41 us (4%)
  other arithmetic  5.7 us (3%)
  Pallas kernels  2.56 us (1%)
    ppermute x39, waiting for transfers between devices, send(): return lax.ppermute(value, AXES, pairs)  89 us
    ppermute x39, starting transfers between devices, send(): return lax.ppermute(value, AXES, pairs)  56 us
    dot_general x24, matrix products, contract(): lax.dot_general(left, right, (((0,), (0,)), ((), ())), preferred_element_...  18.2 us
    unnamed x12, local copies, waits for them, and re-layouts  4.22 us
  transfers between devices with their start and end apart: 39, of which 20 were waited for; matrix products, arithmetic and copies ran while one was open for 12% of the time, Pallas kernels for 1%

profile of v4, /device:TPU:6, one launch (start us, length us, event | category | flops | bytes accessed | tf_op | source)
XLA Modules:
  0.0 178.4 jit_solution(18016916164991925401)
XLA Ops:
  1.0 1.9 %copy-done.1 = s32[128,6144]{1,0:T(8,128)S(1)} copy-done((s32[128,6144]{1,0:T(8,128)S(1)}, s32[128,6144]{1,0:T(8,128)}, u32[]{:S(2)}) %copy-start.1) | copy-done | bytes 3145752
  5.5 2.2 %copy-done = s32[1024,1024]{1,0:T(8,128)S(1)} copy-done((s32[1024,1024]{1,0:T(8,128)S(1)}, s32[1024,1024]{1,0:T(8,128)}, u32[]{:S(2)}) %copy-start) | copy-done | bytes 4194328
  9.5 4.0 %collective-permute-start.1 = (bf16[2,256,512]{2,1,0:T(8,128)(2,1)S(1)}, bf16[2,256,512]{2,1,0:T(8,128)(2,1)S(1)}, u32[]{:S(2)}, u32[]{:S(2)}) collective-permute-start(bf16[2,256,512]{2,1,0:T(8,128)(2,1)S(1)} %pad_maximum_fusion.13), channel_id=1, source_target_pairs={{0,4},{1,5},{2,6},{3,7},{4,0},{5,1},{6,2},{7,3},{8,12},{9,13},{10,... | collective-permute-start | bytes 1572872 | tf_op jit(solution)/shard_map/ppermute | solution.py:28
  15.0 1.7 collective-permute-start.4
  16.7 8.9 %collective-permute-done.1 = bf16[2,256,512]{2,1,0:T(8,128)(2,1)S(1)} collective-permute-done((bf16[2,256,512]{2,1,0:T(8,128)(2,1)S(1)}, bf16[2,256,512]{2,1,0:T(8,128)(2,1)S(1)}, u32[]{:S(2)}, u32[]{:S(2)}) %collective-permute-start.1) | collective-permute-done | bytes 524320 | tf_op jit(solution)/shard_map/ppermute | solution.py:28
  25.5 2.7 %collective-permute-done.3 = bf16[2,256,512]{2,1,0:T(8,128)(2,1)S(1)} collective-permute-done((bf16[2,256,512]{2,1,0:T(8,128)(2,1)S(1)}, bf16[2,256,512]{2,1,0:T(8,128)(2,1)S(1)}, u32[]{:S(2)}, u32[]{:S(2)}) %collective-permute-start.3) | collective-permute-done | bytes 524320 | tf_op jit(solution)/shard_map/ppermute | solution.py:28
  28.4 3.0 %collective-permute-start.6 = (bf16[2,256,512]{2,1,0:T(8,128)(2,1)S(1)}, bf16[2,256,512]{2,1,0:T(8,128)(2,1)S(1)}, u32[]{:S(2)}, u32[]{:S(2)}) collective-permute-start(bf16[2,256,512]{2,1,0:T(8,128)(2,1)S(1)} %collective-permute-done.1), channel_id=1, source_target_pairs={{0,3},{1,0},{2,1},{3,2},{4,7},{5,4},{6,5},{7,6},{8,11},{9,8},{10,9... | collective-permute-start | bytes 1572872 | tf_op jit(solution)/shard_map/ppermute | solution.py:28
  34.0 11.2 %collective-permute-done.7 = bf16[2,256,512]{2,1,0:T(8,128)(2,1)S(1)} collective-permute-done((bf16[2,256,512]{2,1,0:T(8,128)(2,1)S(1)}, bf16[2,256,512]{2,1,0:T(8,128)(2,1)S(1)}, u32[]{:S(2)}, u32[]{:S(2)}) %collective-permute-start.7) | collective-permute-done | bytes 524320 | tf_op jit(solution)/shard_map/ppermute | solution.py:28
  50.4 2.5 %collective-permute-start.8 = (bf16[256,512]{1,0:T(8,128)(2,1)S(1)}, bf16[256,512]{1,0:T(8,128)(2,1)S(1)}, u32[]{:S(2)}, u32[]{:S(2)}) collective-permute-start(bf16[256,512]{1,0:T(8,128)(2,1)S(1)} %pad_maximum_fusion.17), channel_id=1, source_target_pairs={{0,4},{1,5},{2,6},{3,7},{4,0},{5,1},{6,2},{7,3},{8,12},{9,13},{10,... | collective-permute-start | bytes 786440 | tf_op jit(solution)/shard_map/ppermute | solution.py:28
  53.3 2.9 %collective-permute-start.12 = (bf16[512,512]{1,0:T(8,128)(2,1)S(1)}, bf16[512,512]{1,0:T(8,128)(2,1)S(1)}, u32[]{:S(2)}, u32[]{:S(2)}) collective-permute-start(bf16[512,512]{1,0:T(8,128)(2,1)S(1)} %slice_bitcast_fusion.12), channel_id=1, source_target_pairs={{0,3},{1,0},{2,1},{3,2},{4,7},{5,4},{6,5},{7,6},{8,11},{9,8},{10,9... | collective-permute-start | bytes 1572872 | tf_op jit(solution)/shard_map/ppermute | solution.py:28
  56.2 2.2 %collective-permute-done.8 = bf16[256,512]{1,0:T(8,128)(2,1)S(1)} collective-permute-done((bf16[256,512]{1,0:T(8,128)(2,1)S(1)}, bf16[256,512]{1,0:T(8,128)(2,1)S(1)}, u32[]{:S(2)}, u32[]{:S(2)}) %collective-permute-start.8) | collective-permute-done | bytes 262176 | tf_op jit(solution)/shard_map/ppermute | solution.py:28
  59.8 5.2 %collective-permute-done.11 = bf16[512,512]{1,0:T(8,128)(2,1)S(1)} collective-permute-done((bf16[512,512]{1,0:T(8,128)(2,1)S(1)}, bf16[512,512]{1,0:T(8,128)(2,1)S(1)}, u32[]{:S(2)}, u32[]{:S(2)}) %collective-permute-start.11) | collective-permute-done | bytes 524320 | tf_op jit(solution)/shard_map/ppermute | solution.py:28
  65.9 2.4 %collective-permute-start.14 = (bf16[2,512,512]{2,1,0:T(8,128)(2,1)S(1)}, bf16[2,512,512]{2,1,0:T(8,128)(2,1)S(1)}, u32[]{:S(2)}, u32[]{:S(2)}) collective-permute-start(bf16[2,512,512]{2,1,0:T(8,128)(2,1)S(1)} %pad_maximum_fusion.8), channel_id=1, source_target_pairs={{0,3},{1,0},{2,1},{3,2},{4,7},{5,4},{6,5},{7,6},{8,11},{9,8},{10,9... | collective-permute-start | bytes 3145736 | tf_op jit(solution)/shard_map/ppermute | solution.py:28
  72.5 2.5 %collective-permute-start.16 = (f32[2,128,512]{2,1,0:T(8,128)S(1)}, f32[2,128,512]{2,1,0:T(8,128)S(1)}, u32[]{:S(2)}, u32[]{:S(2)}) collective-permute-start(f32[2,128,512]{2,1,0:T(8,128)S(1)} %get-tuple-element.96), channel_id=1, source_target_pairs={{0,32},{1,33},{2,34},{3,35},{4,36},{5,37},{6,38},{7,39},{8,40},{9,... | collective-permute-start | bytes 1572872 | tf_op jit(solution)/shard_map/ppermute | solution.py:28
  76.3 6.4 %collective-permute-done.17 = f32[2,128,512]{2,1,0:T(8,128)S(1)} collective-permute-done((f32[2,128,512]{2,1,0:T(8,128)S(1)}, f32[2,128,512]{2,1,0:T(8,128)S(1)}, u32[]{:S(2)}, u32[]{:S(2)}) %collective-permute-start.17) | collective-permute-done | bytes 524320 | tf_op jit(solution)/shard_map/ppermute | solution.py:28
  83.1 2.2 %collective-permute-done.16 = f32[2,128,512]{2,1,0:T(8,128)S(1)} collective-permute-done((f32[2,128,512]{2,1,0:T(8,128)S(1)}, f32[2,128,512]{2,1,0:T(8,128)S(1)}, u32[]{:S(2)}, u32[]{:S(2)}) %collective-permute-start.16) | collective-permute-done | bytes 524320 | tf_op jit(solution)/shard_map/ppermute | solution.py:28
  85.5 2.5 %collective-permute-start.21 = (f32[2,128,1024]{2,1,0:T(8,128)S(1)}, f32[2,128,1024]{2,1,0:T(8,128)S(1)}, u32[]{:S(2)}, u32[]{:S(2)}) collective-permute-start(f32[2,128,1024]{2,1,0:T(8,128)S(1)} %pad_maximum_fusion.9), channel_id=1, source_target_pairs={{0,32},{1,33},{2,34},{3,35},{4,36},{5,37},{6,38},{7,39},{8,40},{9,... | collective-permute-start | bytes 3145736 | tf_op jit(solution)/shard_map/ppermute | solution.py:28
  90.3 3.0 %collective-permute-start.20 = (bf16[512,512]{1,0:T(8,128)(2,1)S(1)}, bf16[512,512]{1,0:T(8,128)(2,1)S(1)}, u32[]{:S(2)}, u32[]{:S(2)}) collective-permute-start(bf16[512,512]{1,0:T(8,128)(2,1)S(1)} %slice_bitcast_fusion.10), channel_id=1, source_target_pairs={{0,3},{1,0},{2,1},{3,2},{4,7},{5,4},{6,5},{7,6},{8,11},{9,8},{10,9... | collective-permute-start | bytes 1572872 | tf_op jit(solution)/shard_map/ppermute | solution.py:28
  95.5 7.5 %collective-permute-done.22 = f32[2,128,1024]{2,1,0:T(8,128)S(1)} collective-permute-done((f32[2,128,1024]{2,1,0:T(8,128)S(1)}, f32[2,128,1024]{2,1,0:T(8,128)S(1)}, u32[]{:S(2)}, u32[]{:S(2)}) %collective-permute-start.22) | collective-permute-done | bytes 1048608 | tf_op jit(solution)/shard_map/ppermute | solution.py:28
  104.3 3.2 %collective-permute-start.24 = (bf16[1024,512]{1,0:T(8,128)(2,1)S(1)}, bf16[1024,512]{1,0:T(8,128)(2,1)S(1)}, u32[]{:S(2)}, u32[]{:S(2)}) collective-permute-start(bf16[1024,512]{1,0:T(8,128)(2,1)S(1)} %constant_dynamic-update-slice_fusion), channel_id=1, source_target_pairs={{0,3},{1,0},{2,1},{3,2},{4,7},{5,4},{6,5},{7,6},{8,11},{9,8},{10,9... | collective-permute-start | bytes 3145736 | tf_op jit(solution)/shard_map/ppermute | solution.py:28
  110.3 3.7 %collective-permute-start.26 = (f32[2,128,512]{2,1,0:T(8,128)S(1)}, f32[2,128,512]{2,1,0:T(8,128)S(1)}, u32[]{:S(2)}, u32[]{:S(2)}) collective-permute-start(f32[2,128,512]{2,1,0:T(8,128)S(1)} %get-tuple-element.92), channel_id=1, source_target_pairs={{0,32},{1,33},{2,34},{3,35},{4,36},{5,37},{6,38},{7,39},{8,40},{9,... | collective-permute-start | bytes 1572872 | tf_op jit(solution)/shard_map/ppermute | solution.py:28
  114.5 6.3 %collective-permute-done.26 = f32[2,128,512]{2,1,0:T(8,128)S(1)} collective-permute-done((f32[2,128,512]{2,1,0:T(8,128)S(1)}, f32[2,128,512]{2,1,0:T(8,128)S(1)}, u32[]{:S(2)}, u32[]{:S(2)}) %collective-permute-start.26) | collective-permute-done | bytes 524320 | tf_op jit(solution)/shard_map/ppermute | solution.py:28
  120.7 3.7 %collective-permute-done.27 = f32[2,128,512]{2,1,0:T(8,128)S(1)} collective-permute-done((f32[2,128,512]{2,1,0:T(8,128)S(1)}, f32[2,128,512]{2,1,0:T(8,128)S(1)}, u32[]{:S(2)}, u32[]{:S(2)}) %collective-permute-start.27) | collective-permute-done | bytes 524320 | tf_op jit(solution)/shard_map/ppermute | solution.py:28
  127.0 3.4 %collective-permute-start.32 = (f32[2,128,1024]{2,1,0:T(8,128)S(1)}, f32[2,128,1024]{2,1,0:T(8,128)S(1)}, u32[]{:S(2)}, u32[]{:S(2)}) collective-permute-start(f32[2,128,1024]{2,1,0:T(8,128)S(1)} %pad_maximum_fusion.11), channel_id=1, source_target_pairs={{0,32},{1,33},{2,34},{3,35},{4,36},{5,37},{6,38},{7,39},{8,40},{9,... | collective-permute-start | bytes 3145736 | tf_op jit(solution)/shard_map/ppermute | solution.py:28
  130.6 3.3 %collective-permute-start.30 = (bf16[512,512]{1,0:T(8,128)(2,1)S(1)}, bf16[512,512]{1,0:T(8,128)(2,1)S(1)}, u32[]{:S(2)}, u32[]{:S(2)}) collective-permute-start(bf16[512,512]{1,0:T(8,128)(2,1)S(1)} %slice.290), channel_id=1, source_target_pairs={{0,3},{1,0},{2,1},{3,2},{4,7},{5,4},{6,5},{7,6},{8,11},{9,8},{10,9... | collective-permute-start | bytes 1572872 | tf_op jit(solution)/shard_map/ppermute | solution.py:28
  139.7 6.1 %collective-permute-done.29 = bf16[512,512]{1,0:T(8,128)(2,1)S(1)} collective-permute-done((bf16[512,512]{1,0:T(8,128)(2,1)S(1)}, bf16[512,512]{1,0:T(8,128)(2,1)S(1)}, u32[]{:S(2)}, u32[]{:S(2)}) %collective-permute-start.29) | collective-permute-done | bytes 524320 | tf_op jit(solution)/shard_map/ppermute | solution.py:28
  145.8 5.3 %collective-permute-done.31 = f32[128,1024]{1,0:T(8,128)S(1)} collective-permute-done((f32[128,1024]{1,0:T(8,128)S(1)}, f32[128,1024]{1,0:T(8,128)S(1)}, u32[]{:S(2)}, u32[]{:S(2)}) %collective-permute-start.31) | collective-permute-done | bytes 524320 | tf_op jit(solution)/shard_map/ppermute | solution.py:28
  152.6 1.8 %collective-permute-start.34 = (f32[128,512]{1,0:T(8,128)S(1)}, f32[128,512]{1,0:T(8,128)S(1)}, u32[]{:S(2)}, u32[]{:S(2)}) collective-permute-start(f32[128,512]{1,0:T(8,128)S(1)} %get-tuple-element.106), channel_id=1, source_target_pairs={{0,32},{1,33},{2,34},{3,35},{4,36},{5,37},{6,38},{7,39},{8,40},{9,... | collective-permute-start | bytes 786440 | tf_op jit(solution)/shard_map/ppermute | solution.py:28
  154.7 4.9 %collective-permute-done.34 = f32[128,512]{1,0:T(8,128)S(1)} collective-permute-done((f32[128,512]{1,0:T(8,128)S(1)}, f32[128,512]{1,0:T(8,128)S(1)}, u32[]{:S(2)}, u32[]{:S(2)}) %collective-permute-start.34) | collective-permute-done | bytes 262176 | tf_op jit(solution)/shard_map/ppermute | solution.py:28
  159.7 2.4 %collective-permute-done.35 = f32[128,512]{1,0:T(8,128)S(1)} collective-permute-done((f32[128,512]{1,0:T(8,128)S(1)}, f32[128,512]{1,0:T(8,128)S(1)}, u32[]{:S(2)}, u32[]{:S(2)}) %collective-permute-start.35) | collective-permute-done | bytes 262176 | tf_op jit(solution)/shard_map/ppermute | solution.py:28
  165.9 7.4 %collective-permute-done.36 = f32[128,1024]{1,0:T(8,128)S(1)} collective-permute-done((f32[128,1024]{1,0:T(8,128)S(1)}, f32[128,1024]{1,0:T(8,128)S(1)}, u32[]{:S(2)}, u32[]{:S(2)}) %collective-permute-start.36) | collective-permute-done | bytes 524320 | tf_op jit(solution)/shard_map/ppermute | solution.py:28
  174.2 2.8 %collective-permute-done.38 = f32[128,1024]{1,0:T(8,128)S(1)} collective-permute-done((f32[128,1024]{1,0:T(8,128)S(1)}, f32[128,1024]{1,0:T(8,128)S(1)}, u32[]{:S(2)}, u32[]{:S(2)}) %collective-permute-start.38) | collective-permute-done | bytes 524320 | tf_op jit(solution)/shard_map/ppermute | solution.py:28
  (146 shorter events, 48.8 us)
Async XLA Ops:
  8.8 19.5 %collective-permute-start.2 = (bf16[4,2,128,1024]{3,2,1,0:T(8,128)(2,1)S(1)}, bf16[4,2,128,1024]{3,2,1,0:T(8,128)(2,1)S(1)}, u32[]{:S(2)}, u32[]{:S(2)}) collective-permute-start(bf16[4,2,128,1024]{3,2,1,0:T(8,128)(2,1)S(1)} %bitcast.171), channel_id=1, source_target_pairs={{0,8},{1,9},{2,10},{3,11},{4,12},{5,13},{6,14},{7,15},{8,0},{9,1},... | collective-permute-start | bytes 6291464 | tf_op jit(solution)/shard_map/ppermute | solution.py:28
  9.5 16.1 %collective-permute-start.1 = (bf16[2,256,512]{2,1,0:T(8,128)(2,1)S(1)}, bf16[2,256,512]{2,1,0:T(8,128)(2,1)S(1)}, u32[]{:S(2)}, u32[]{:S(2)}) collective-permute-start(bf16[2,256,512]{2,1,0:T(8,128)(2,1)S(1)} %pad_maximum_fusion.13), channel_id=1, source_target_pairs={{0,4},{1,5},{2,6},{3,7},{4,0},{5,1},{6,2},{7,3},{8,12},{9,13},{10,... | collective-permute-start | bytes 1572872 | tf_op jit(solution)/shard_map/ppermute | solution.py:28
  13.4 14.8 %collective-permute-start.3 = (bf16[2,256,512]{2,1,0:T(8,128)(2,1)S(1)}, bf16[2,256,512]{2,1,0:T(8,128)(2,1)S(1)}, u32[]{:S(2)}, u32[]{:S(2)}) collective-permute-start(bf16[2,256,512]{2,1,0:T(8,128)(2,1)S(1)} %pad_maximum_fusion.13), channel_id=1, source_target_pairs={{0,1},{1,2},{2,3},{3,0},{4,5},{5,6},{6,7},{7,4},{8,9},{9,10},{10,1... | collective-permute-start | bytes 1572872 | tf_op jit(solution)/shard_map/ppermute | solution.py:28
  15.0 13.3 %collective-permute-start.4 = (bf16[2,256,512]{2,1,0:T(8,128)(2,1)S(1)}, bf16[2,256,512]{2,1,0:T(8,128)(2,1)S(1)}, u32[]{:S(2)}, u32[]{:S(2)}) collective-permute-start(bf16[2,256,512]{2,1,0:T(8,128)(2,1)S(1)} %pad_maximum_fusion.13), channel_id=1, source_target_pairs={{0,3},{1,0},{2,1},{3,2},{4,7},{5,4},{6,5},{7,6},{8,11},{9,8},{10,9... | collective-permute-start | bytes 1572872 | tf_op jit(solution)/shard_map/ppermute | solution.py:28
  28.4 16.9 %collective-permute-start.6 = (bf16[2,256,512]{2,1,0:T(8,128)(2,1)S(1)}, bf16[2,256,512]{2,1,0:T(8,128)(2,1)S(1)}, u32[]{:S(2)}, u32[]{:S(2)}) collective-permute-start(bf16[2,256,512]{2,1,0:T(8,128)(2,1)S(1)} %collective-permute-done.1), channel_id=1, source_target_pairs={{0,3},{1,0},{2,1},{3,2},{4,7},{5,4},{6,5},{7,6},{8,11},{9,8},{10,9... | collective-permute-start | bytes 1572872 | tf_op jit(solution)/shard_map/ppermute | solution.py:28
  31.4 14.0 %collective-permute-start.5 = (bf16[2,256,512]{2,1,0:T(8,128)(2,1)S(1)}, bf16[2,256,512]{2,1,0:T(8,128)(2,1)S(1)}, u32[]{:S(2)}, u32[]{:S(2)}) collective-permute-start(bf16[2,256,512]{2,1,0:T(8,128)(2,1)S(1)} %collective-permute-done.1), channel_id=1, source_target_pairs={{0,1},{1,2},{2,3},{3,0},{4,5},{5,6},{6,7},{7,4},{8,9},{9,10},{10,1... | collective-permute-start | bytes 1572872 | tf_op jit(solution)/shard_map/ppermute | solution.py:28
  31.5 13.7 %collective-permute-start.7 = (bf16[2,256,512]{2,1,0:T(8,128)(2,1)S(1)}, bf16[2,256,512]{2,1,0:T(8,128)(2,1)S(1)}, u32[]{:S(2)}, u32[]{:S(2)}) collective-permute-start(bf16[2,256,512]{2,1,0:T(8,128)(2,1)S(1)} %pad_maximum_fusion.14), channel_id=1, source_target_pairs={{0,4},{1,5},{2,6},{3,7},{4,0},{5,1},{6,2},{7,3},{8,12},{9,13},{10,... | collective-permute-start | bytes 1572872 | tf_op jit(solution)/shard_map/ppermute | solution.py:28
  45.5 13.0 %collective-permute-start.9 = (bf16[256,512]{1,0:T(8,128)(2,1)S(1)}, bf16[256,512]{1,0:T(8,128)(2,1)S(1)}, u32[]{:S(2)}, u32[]{:S(2)}) collective-permute-start(bf16[256,512]{1,0:T(8,128)(2,1)S(1)} %pad_maximum_fusion.18), channel_id=1, source_target_pairs={{0,16},{1,17},{2,18},{3,19},{4,20},{5,21},{6,22},{7,23},{8,24},{9,... | collective-permute-start | bytes 786440 | tf_op jit(solution)/shard_map/ppermute | solution.py:28
  46.6 13.2 %collective-permute-start.10 = (bf16[256,512]{1,0:T(8,128)(2,1)S(1)}, bf16[256,512]{1,0:T(8,128)(2,1)S(1)}, u32[]{:S(2)}, u32[]{:S(2)}) collective-permute-start(bf16[256,512]{1,0:T(8,128)(2,1)S(1)} %pad_maximum_fusion.18), channel_id=1, source_target_pairs={{0,20},{1,21},{2,22},{3,23},{4,16},{5,17},{6,18},{7,19},{8,28},{9,... | collective-permute-start | bytes 786440 | tf_op jit(solution)/shard_map/ppermute | solution.py:28
  52.9 12.2 %collective-permute-start.11 = (bf16[512,512]{1,0:T(8,128)(2,1)S(1)}, bf16[512,512]{1,0:T(8,128)(2,1)S(1)}, u32[]{:S(2)}, u32[]{:S(2)}) collective-permute-start(bf16[512,512]{1,0:T(8,128)(2,1)S(1)} %slice_bitcast_fusion.13), channel_id=1, source_target_pairs={{0,1},{1,2},{2,3},{3,0},{4,5},{5,6},{6,7},{7,4},{8,9},{9,10},{10,1... | collective-permute-start | bytes 1572872 | tf_op jit(solution)/shard_map/ppermute | solution.py:28
  53.3 11.8 %collective-permute-start.12 = (bf16[512,512]{1,0:T(8,128)(2,1)S(1)}, bf16[512,512]{1,0:T(8,128)(2,1)S(1)}, u32[]{:S(2)}, u32[]{:S(2)}) collective-permute-start(bf16[512,512]{1,0:T(8,128)(2,1)S(1)} %slice_bitcast_fusion.12), channel_id=1, source_target_pairs={{0,3},{1,0},{2,1},{3,2},{4,7},{5,4},{6,5},{7,6},{8,11},{9,8},{10,9... | collective-permute-start | bytes 1572872 | tf_op jit(solution)/shard_map/ppermute | solution.py:28
  65.1 23.0 %collective-permute-start.13 = (bf16[2,512,512]{2,1,0:T(8,128)(2,1)S(1)}, bf16[2,512,512]{2,1,0:T(8,128)(2,1)S(1)}, u32[]{:S(2)}, u32[]{:S(2)}) collective-permute-start(bf16[2,512,512]{2,1,0:T(8,128)(2,1)S(1)} %pad_maximum_fusion.8), channel_id=1, source_target_pairs={{0,1},{1,2},{2,3},{3,0},{4,5},{5,6},{6,7},{7,4},{8,9},{9,10},{10,1... | collective-permute-start | bytes 3145736 | tf_op jit(solution)/shard_map/ppermute | solution.py:28
  65.9 22.1 %collective-permute-start.14 = (bf16[2,512,512]{2,1,0:T(8,128)(2,1)S(1)}, bf16[2,512,512]{2,1,0:T(8,128)(2,1)S(1)}, u32[]{:S(2)}, u32[]{:S(2)}) collective-permute-start(bf16[2,512,512]{2,1,0:T(8,128)(2,1)S(1)} %pad_maximum_fusion.8), channel_id=1, source_target_pairs={{0,3},{1,0},{2,1},{3,2},{4,7},{5,4},{6,5},{7,6},{8,11},{9,8},{10,9... | collective-permute-start | bytes 3145736 | tf_op jit(solution)/shard_map/ppermute | solution.py:28
  69.9 12.8 %collective-permute-start.17 = (f32[2,128,512]{2,1,0:T(8,128)S(1)}, f32[2,128,512]{2,1,0:T(8,128)S(1)}, u32[]{:S(2)}, u32[]{:S(2)}) collective-permute-start(f32[2,128,512]{2,1,0:T(8,128)S(1)} %get-tuple-element.95), channel_id=1, source_target_pairs={{0,96},{1,97},{2,98},{3,99},{4,100},{5,101},{6,102},{7,103},{8,104... | collective-permute-start | bytes 1572872 | tf_op jit(solution)/shard_map/ppermute | solution.py:28
  72.5 12.9 %collective-permute-start.16 = (f32[2,128,512]{2,1,0:T(8,128)S(1)}, f32[2,128,512]{2,1,0:T(8,128)S(1)}, u32[]{:S(2)}, u32[]{:S(2)}) collective-permute-start(f32[2,128,512]{2,1,0:T(8,128)S(1)} %get-tuple-element.96), channel_id=1, source_target_pairs={{0,32},{1,33},{2,34},{3,35},{4,36},{5,37},{6,38},{7,39},{8,40},{9,... | collective-permute-start | bytes 1572872 | tf_op jit(solution)/shard_map/ppermute | solution.py:28
  75.0 13.0 %collective-permute-start.15 = (bf16[1,2,128,1024]{3,2,1,0:T(8,128)(2,1)S(1)}, bf16[1,2,128,1024]{3,2,1,0:T(8,128)(2,1)S(1)}, u32[]{:S(2)}, u32[]{:S(2)}) collective-permute-start(bf16[1,2,128,1024]{3,2,1,0:T(8,128)(2,1)S(1)} %slice.264), channel_id=1, source_target_pairs={{0,16},{1,17},{2,18},{3,19},{4,20},{5,21},{6,22},{7,23},{8,24},{9,... | collective-permute-start | bytes 1572872 | tf_op jit(solution)/shard_map/ppermute | solution.py:28
  82.9 20.1 %collective-permute-start.22 = (f32[2,128,1024]{2,1,0:T(8,128)S(1)}, f32[2,128,1024]{2,1,0:T(8,128)S(1)}, u32[]{:S(2)}, u32[]{:S(2)}) collective-permute-start(f32[2,128,1024]{2,1,0:T(8,128)S(1)} %pad_maximum_fusion.10), channel_id=1, source_target_pairs={{0,96},{1,97},{2,98},{3,99},{4,100},{5,101},{6,102},{7,103},{8,104... | collective-permute-start | bytes 3145736 | tf_op jit(solution)/shard_map/ppermute | solution.py:28
  85.5 18.7 %collective-permute-start.21 = (f32[2,128,1024]{2,1,0:T(8,128)S(1)}, f32[2,128,1024]{2,1,0:T(8,128)S(1)}, u32[]{:S(2)}, u32[]{:S(2)}) collective-permute-start(f32[2,128,1024]{2,1,0:T(8,128)S(1)} %pad_maximum_fusion.9), channel_id=1, source_target_pairs={{0,32},{1,33},{2,34},{3,35},{4,36},{5,37},{6,38},{7,39},{8,40},{9,... | collective-permute-start | bytes 3145736 | tf_op jit(solution)/shard_map/ppermute | solution.py:28
  88.9 15.3 %collective-permute-start.18 = (bf16[1,2,128,1024]{3,2,1,0:T(8,128)(2,1)S(1)}, bf16[1,2,128,1024]{3,2,1,0:T(8,128)(2,1)S(1)}, u32[]{:S(2)}, u32[]{:S(2)}) collective-permute-start(bf16[1,2,128,1024]{3,2,1,0:T(8,128)(2,1)S(1)} %slice.267), channel_id=1, source_target_pairs={{0,16},{1,17},{2,18},{3,19},{4,20},{5,21},{6,22},{7,23},{8,24},{9,... | collective-permute-start | bytes 1572872 | tf_op jit(solution)/shard_map/ppermute | solution.py:28
  90.0 14.2 %collective-permute-start.19 = (bf16[512,512]{1,0:T(8,128)(2,1)S(1)}, bf16[512,512]{1,0:T(8,128)(2,1)S(1)}, u32[]{:S(2)}, u32[]{:S(2)}) collective-permute-start(bf16[512,512]{1,0:T(8,128)(2,1)S(1)} %slice_bitcast_fusion.11), channel_id=1, source_target_pairs={{0,1},{1,2},{2,3},{3,0},{4,5},{5,6},{6,7},{7,4},{8,9},{9,10},{10,1... | collective-permute-start | bytes 1572872 | tf_op jit(solution)/shard_map/ppermute | solution.py:28
  90.3 13.9 %collective-permute-start.20 = (bf16[512,512]{1,0:T(8,128)(2,1)S(1)}, bf16[512,512]{1,0:T(8,128)(2,1)S(1)}, u32[]{:S(2)}, u32[]{:S(2)}) collective-permute-start(bf16[512,512]{1,0:T(8,128)(2,1)S(1)} %slice_bitcast_fusion.10), channel_id=1, source_target_pairs={{0,3},{1,0},{2,1},{3,2},{4,7},{5,4},{6,5},{7,6},{8,11},{9,8},{10,9... | collective-permute-start | bytes 1572872 | tf_op jit(solution)/shard_map/ppermute | solution.py:28
  104.2 20.6 %collective-permute-start.23 = (bf16[1024,512]{1,0:T(8,128)(2,1)S(1)}, bf16[1024,512]{1,0:T(8,128)(2,1)S(1)}, u32[]{:S(2)}, u32[]{:S(2)}) collective-permute-start(bf16[1024,512]{1,0:T(8,128)(2,1)S(1)} %constant_dynamic-update-slice_fusion), channel_id=1, source_target_pairs={{0,1},{1,2},{2,3},{3,0},{4,5},{5,6},{6,7},{7,4},{8,9},{9,10},{10,1... | collective-permute-start | bytes 3145736 | tf_op jit(solution)/shard_map/ppermute | solution.py:28
  104.3 20.5 %collective-permute-start.24 = (bf16[1024,512]{1,0:T(8,128)(2,1)S(1)}, bf16[1024,512]{1,0:T(8,128)(2,1)S(1)}, u32[]{:S(2)}, u32[]{:S(2)}) collective-permute-start(bf16[1024,512]{1,0:T(8,128)(2,1)S(1)} %constant_dynamic-update-slice_fusion), channel_id=1, source_target_pairs={{0,3},{1,0},{2,1},{3,2},{4,7},{5,4},{6,5},{7,6},{8,11},{9,8},{10,9... | collective-permute-start | bytes 3145736 | tf_op jit(solution)/shard_map/ppermute | solution.py:28
  107.6 17.2 %collective-permute-start.25 = (bf16[2,2,128,1024]{3,2,1,0:T(8,128)(2,1)S(1)}, bf16[2,2,128,1024]{3,2,1,0:T(8,128)(2,1)S(1)}, u32[]{:S(2)}, u32[]{:S(2)}) collective-permute-start(bf16[2,2,128,1024]{3,2,1,0:T(8,128)(2,1)S(1)} %slice.278), channel_id=1, source_target_pairs={{0,16},{1,17},{2,18},{3,19},{4,20},{5,21},{6,22},{7,23},{8,24},{9,... | collective-permute-start | bytes 3145736 | tf_op jit(solution)/shard_map/ppermute | solution.py:28
  126.2 28.6 %collective-permute-start.33 = (f32[2,128,1024]{2,1,0:T(8,128)S(1)}, f32[2,128,1024]{2,1,0:T(8,128)S(1)}, u32[]{:S(2)}, u32[]{:S(2)}) collective-permute-start(f32[2,128,1024]{2,1,0:T(8,128)S(1)} %pad_maximum_fusion.12), channel_id=1, source_target_pairs={{0,96},{1,97},{2,98},{3,99},{4,100},{5,101},{6,102},{7,103},{8,104... | collective-permute-start | bytes 3145736 | tf_op jit(solution)/shard_map/ppermute | solution.py:28
  127.0 27.7 %collective-permute-start.32 = (f32[2,128,1024]{2,1,0:T(8,128)S(1)}, f32[2,128,1024]{2,1,0:T(8,128)S(1)}, u32[]{:S(2)}, u32[]{:S(2)}) collective-permute-start(f32[2,128,1024]{2,1,0:T(8,128)S(1)} %pad_maximum_fusion.11), channel_id=1, source_target_pairs={{0,32},{1,33},{2,34},{3,35},{4,36},{5,37},{6,38},{7,39},{8,40},{9,... | collective-permute-start | bytes 3145736 | tf_op jit(solution)/shard_map/ppermute | solution.py:28
  130.4 15.3 %collective-permute-start.29 = (bf16[512,512]{1,0:T(8,128)(2,1)S(1)}, bf16[512,512]{1,0:T(8,128)(2,1)S(1)}, u32[]{:S(2)}, u32[]{:S(2)}) collective-permute-start(bf16[512,512]{1,0:T(8,128)(2,1)S(1)} %slice.286), channel_id=1, source_target_pairs={{0,1},{1,2},{2,3},{3,0},{4,5},{5,6},{6,7},{7,4},{8,9},{9,10},{10,1... | collective-permute-start | bytes 1572872 | tf_op jit(solution)/shard_map/ppermute | solution.py:28
  130.6 15.2 %collective-permute-start.30 = (bf16[512,512]{1,0:T(8,128)(2,1)S(1)}, bf16[512,512]{1,0:T(8,128)(2,1)S(1)}, u32[]{:S(2)}, u32[]{:S(2)}) collective-permute-start(bf16[512,512]{1,0:T(8,128)(2,1)S(1)} %slice.290), channel_id=1, source_target_pairs={{0,3},{1,0},{2,1},{3,2},{4,7},{5,4},{6,5},{7,6},{8,11},{9,8},{10,9... | collective-permute-start | bytes 1572872 | tf_op jit(solution)/shard_map/ppermute | solution.py:28
  137.5 13.6 %collective-permute-start.31 = (f32[128,1024]{1,0:T(8,128)S(1)}, f32[128,1024]{1,0:T(8,128)S(1)}, u32[]{:S(2)}, u32[]{:S(2)}) collective-permute-start(f32[128,1024]{1,0:T(8,128)S(1)} %slice_bitcast_fusion.4), channel_id=1, source_target_pairs={{0,16},{1,17},{2,18},{3,19},{4,20},{5,21},{6,22},{7,23},{8,24},{9,... | collective-permute-start | bytes 1572872 | tf_op jit(solution)/shard_map/ppermute | solution.py:28
  162.3 10.9 %collective-permute-start.36 = (f32[128,1024]{1,0:T(8,128)S(1)}, f32[128,1024]{1,0:T(8,128)S(1)}, u32[]{:S(2)}, u32[]{:S(2)}) collective-permute-start(f32[128,1024]{1,0:T(8,128)S(1)} %slice_bitcast_fusion.2), channel_id=1, source_target_pairs={{0,16},{1,17},{2,18},{3,19},{4,20},{5,21},{6,22},{7,23},{8,24},{9,... | collective-permute-start | bytes 1572872 | tf_op jit(solution)/shard_map/ppermute | solution.py:28
  163.6 10.6 %collective-permute-start.37 = (f32[128,1024]{1,0:T(8,128)S(1)}, f32[128,1024]{1,0:T(8,128)S(1)}, u32[]{:S(2)}, u32[]{:S(2)}) collective-permute-start(f32[128,1024]{1,0:T(8,128)S(1)} %pad_maximum_fusion.15), channel_id=1, source_target_pairs={{0,32},{1,33},{2,34},{3,35},{4,36},{5,37},{6,38},{7,39},{8,40},{9,... | collective-permute-start | bytes 1572872 | tf_op jit(solution)/shard_map/ppermute | solution.py:28
  164.5 12.6 %collective-permute-start.38 = (f32[128,1024]{1,0:T(8,128)S(1)}, f32[128,1024]{1,0:T(8,128)S(1)}, u32[]{:S(2)}, u32[]{:S(2)}) collective-permute-start(f32[128,1024]{1,0:T(8,128)S(1)} %pad_maximum_fusion.16), channel_id=1, source_target_pairs={{0,96},{1,97},{2,98},{3,99},{4,100},{5,101},{6,102},{7,103},{8,104... | collective-permute-start | bytes 1572872 | tf_op jit(solution)/shard_map/ppermute | solution.py:28
  (10 other events, 62.4 us)
